TPU v7x, 32 devices: a whole 2x2x4 slice. The times are simulated.
32 devices in a mesh: seq: 16 (over z, y, x), head: 2 (over core).
Axes of the slice: x: 2, y: 2, z: 4, core: 2. Of those that a mesh axis runs over, the one named last changes fastest.
Arguments:
- inner_acts: bfloat16 [4096, 8192], P('seq', 'head'), may hold values from -0.4375 to 0.4375
- out_grad: bfloat16 [4096, 8192], P('seq', 'head'), may hold values from -0.4375 to 0.4375
- write_proj: bfloat16 [4096, 128], P('seq'), may hold values from -3 to 3
- read_proj: bfloat16 [4096, 128], P('seq'), may hold values from -3 to 3
- log_decay: float32 [4096, 64], P('seq', 'head'), may hold values from -2.5 to 0, as said below
- w_in: bfloat16 [4096, 8192], P('seq', 'head'), may hold values from -0.09375 to 0.09375
Outputs:
- input_grad: bfloat16 [4096, 4096], P('seq', 'head')
- act_grad: bfloat16 [4096, 8192], P('seq', 'head')
- write_grad: float32 [4096, 128], P('seq')
- read_grad: float32 [4096, 128], P('seq')
Inputs may be any that keep to these rules, and one draw needn't show every extreme that they name: `log_decay`: natural log of a decay factor of each head at each token; every entry is negative.
All inputs are finite; a program needn't handle non-finite values.
Results may differ from a plain program's by a relative error of at most 0.019.
Values may be sent and summed in bfloat16 or wider, within the bound.
No kernel may reach another device: no remote copies, remote signals or barrier semaphores. Data moves between devices by JAX's collectives and lax.ppermute only.
A program may use at most 192 MiB of HBM per device.

v0:
```python
import functools

import jax
import jax.numpy as jnp
from jax import lax
from jax.experimental import pallas as pl
from jax.experimental.pallas import tpu as pltpu
from jax.sharding import PartitionSpec as P

RING = 4
LANES = 128
EXTRA = 16
NT = (((1,), (1,)), ((), ()))
TN = (((0,), (0,)), ((), ()))
NN = (((1,), (0,)), ((), ()))
bf16, f32 = jnp.bfloat16, jnp.float32


def mm(a, b, dims):
    return lax.dot_general(a, b, dims, preferred_element_type=f32)


def mm_exact(a, b, dims):
    return lax.dot_general(a, b, dims, precision=lax.Precision.HIGHEST, preferred_element_type=f32)


def spread(columns, width):
    rows = columns.shape[0]
    return jnp.concatenate(
        [jnp.broadcast_to(columns[:, h : h + 1], (rows, width)) for h in range(columns.shape[1])],
        axis=1,
    )


def iota(shape, axis):
    return lax.broadcasted_iota(jnp.int32, shape, axis)


def three_parts(value):
    first = value.astype(bf16).astype(f32)
    second = (value - first).astype(bf16).astype(f32)
    return first, second, value - first - second


def cumulate(n_heads, log_tiles, cum, cum_t):
    parts = jnp.concatenate([tile[...] for tile in log_tiles], axis=0)
    rows = parts.shape[0]
    source, head = iota((LANES, LANES), 0), iota((LANES, LANES), 1)
    pick = (source < 3 * n_heads) & (lax.rem(source, n_heads) == head)
    logs = mm(parts, pick.astype(f32).astype(bf16), NN)
    upto = (iota((rows, rows), 0) <= iota((rows, rows), 1)).astype(f32)
    cum[...] = mm_exact(upto, logs, TN)
    if cum_t is not None:
        cum_t[...] = mm_exact(logs, upto, TN)


def group_of(value, g, heads, axis):
    shift = lax.rem(LANES - g * heads, LANES)
    value = pltpu.roll(value, shift, axis)
    return value[:, :heads] if axis == 1 else value[:heads]


def diagonal(heads, half, lo, col, row, each):
    later = iota((half, half), 1) >= iota((half, half), 0)
    for h in range(heads):
        log = row[h : h + 1, lo : lo + half] - col[lo : lo + half, h : h + 1]
        each(h, jnp.exp(jnp.where(later, log, -jnp.inf)))


def cumulate_own(log_t, cum, cum_t):
    n_heads, rows = log_t.shape
    logs = jnp.concatenate([log_t[...], jnp.zeros((LANES - n_heads, rows), f32)], axis=0)
    upto = (iota((rows, rows), 0) <= iota((rows, rows), 1)).astype(f32)
    cum[...] = mm_exact(upto, logs, (((0,), (1,)), ((), ())))
    if cum_t is not None:
        cum_t[...] = mm_exact(logs, upto, NN)


def edge_kernel(n_heads, at, x, dy, b, c, log_t, *refs):
    messages, cum = refs[:RING], refs[RING]
    g = pl.program_id(0)
    heads = n_heads // RING
    rows = x.shape[0]
    width = x.shape[1] // heads
    n = b.shape[1]

    @pl.when(g == 0)
    def _():
        cumulate_own(log_t, cum, None)

    col = group_of(cum[...], g, heads, 1)
    last = col[rows - 1 : rows, :]
    tailed = (x[...].astype(f32) * spread(jnp.exp(last - col), width)).astype(bf16)
    decayed = (dy[...].astype(f32) * spread(jnp.exp(col), width)).astype(bf16)
    ends = mm(b[...], tailed, TN).astype(bf16)
    fronts = mm(c[...], decayed, TN).astype(bf16)
    log = spread(last, width)
    for j in range(RING):

        @pl.when(lax.bitwise_xor(at[0], g) == j)
        def _():
            messages[j][:n] = ends
            messages[j][n : 2 * n] = fronts
            write_log(messages[j], log)


def pack_kernel(n_heads, dy, b, c, log_t, out):
    rows, columns = dy.shape
    fill = jnp.zeros((LANES - 3 * n_heads, rows), f32)
    logs = jnp.concatenate([*three_parts(log_t[...]), fill], axis=0)
    out[:, :columns] = dy[...]
    out[:, columns : columns + LANES] = b[...]
    out[:, columns + LANES : columns + 2 * LANES] = c[...]
    out[:, columns + 2 * LANES :] = logs.T.astype(bf16)


def own_kernel(n_heads, x, dy, b, c, log_t, write_local, read_local, total, cum, cum_t):
    g = pl.program_id(0)
    heads = n_heads // RING
    rows = x.shape[0]
    half = rows // 2
    width = x.shape[1] // heads

    @pl.when(g == 0)
    def _():
        total[...] = jnp.zeros_like(total)
        cumulate_own(log_t, cum, cum_t)

    col, row = group_of(cum[...], g, heads, 1), group_of(cum_t[...], g, heads, 0)
    mid = col[half - 1 : half, :]
    for i in range(2):
        lo = i * half
        parts = []

        def add(h, decay):
            span = slice(h * width, (h + 1) * width)
            parts.append(decay * mm(x[lo : lo + half, span], dy[lo : lo + half, span], NT))

        diagonal(heads, half, lo, col, row, add)
        total[lo : lo + half, lo : lo + half] += sum(parts)
    early = (x[:half].astype(f32) * spread(jnp.exp(mid - col[:half]), width)).astype(bf16)
    late = (dy[half:].astype(f32) * spread(jnp.exp(col[half:] - mid), width)).astype(bf16)
    total[:half, half:] += mm(early, late, NT)

    @pl.when(g == pl.num_programs(0) - 1)
    def _():
        write_local[...] = mm_exact(total[...], c[...].astype(f32), NN)
        read_local[...] = mm_exact(total[...], b[...].astype(f32), TN)


def block_kernel(n_heads, top, bottom, *refs):
    tiles, (act, fronts, log_row, cum_out, cum_t) = refs[:6], refs[6:]
    b = jnp.concatenate([tiles[0][...], tiles[1][...]], axis=0)
    c = jnp.concatenate([tiles[2][...], tiles[3][...]], axis=0)
    g = pl.program_id(0)
    heads = n_heads // RING
    half = top.shape[0]
    rows = 2 * half
    width = top.shape[1] // heads

    @pl.when(g == 0)
    def _():
        cumulate(n_heads, tiles[4:], cum_out, cum_t)

    col, row = group_of(cum_out[...], g, heads, 1), group_of(cum_t[...], g, heads, 0)
    mid, last = col[half - 1 : half, :], col[rows - 1 : rows, :]
    log_row[...] = spread(last, width)
    scores = mm(b, c, NT)
    late_f = bottom[...].astype(f32) * spread(jnp.exp(col[half:] - mid), width)
    late = late_f.astype(bf16)
    first = (top[...].astype(f32) * spread(jnp.exp(col[:half]), width)).astype(bf16)
    second = (late_f * spread(jnp.exp(mid), width)).astype(bf16)
    fronts[0] = (mm(c[:half], first, TN) + mm(c[half:], second, TN)).astype(bf16)
    cross = mm(scores[:half, half:].astype(bf16), late, NN)
    to_mid = jnp.exp(mid - col[:half])
    for i, dy in enumerate((top, bottom)):
        lo = i * half
        score = scores[lo : lo + half, lo : lo + half]

        def put(h, decay):
            span = slice(h * width, (h + 1) * width)
            out = mm((decay * score).astype(bf16), dy[:, span], NN)
            if i == 0:
                out += cross[:, span] * to_mid[:, h : h + 1]
            act[lo : lo + half, span] = out.astype(act.dtype)

        diagonal(heads, half, lo, col, row, put)


def log_over(p, logs, wanted):
    total = jnp.zeros_like(logs[0])
    for k in range(RING):
        total += jnp.where(wanted(lax.bitwise_xor(p, k)), logs[k], 0.0)
    return total


def combine_kernel(at, *refs):
    parts, (state_out, grad_out) = refs[:RING], refs[RING:]
    n = state_out.shape[0] - EXTRA
    logs = [log_of(part) for part in parts]
    p = at[0]
    state, grad = 0.0, 0.0
    for j in range(RING):
        own = lax.bitwise_xor(p, j)
        state += parts[j][:n].astype(f32) * jnp.exp(log_over(p, logs, lambda k: k > own))
        grad += parts[j][n : 2 * n].astype(f32) * jnp.exp(log_over(p, logs, lambda k: k < own))
    for out, value in ((state_out, state), (grad_out, grad)):
        out[:n] = value.astype(bf16)
        write_log(out, sum(logs))


def write_log(out, log):
    n, width = out.shape
    row = iota((EXTRA, width), 0)
    rows = jnp.zeros((EXTRA, width), f32)
    for i, part in enumerate(three_parts(log)):
        rows = jnp.where(row == i, part, rows)
    out[n - EXTRA :] = rows.astype(bf16)


def log_of(message):
    n = message.shape[0] - EXTRA
    tail = message[n:].astype(f32)
    return tail[0:1] + tail[1:2] + tail[2:3]


def merge_kernel(*refs):
    for near, far, out in ((*refs[:2], refs[4]), (*refs[2:4], refs[5])):
        n = near.shape[0] - EXTRA
        log = log_of(near)
        out[:n] = (near[:n].astype(f32) + far[:n].astype(f32) * jnp.exp(log)).astype(bf16)
        write_log(out, log + log_of(far))


def ring_kernel(at, *refs):
    fronts, logs, outs = refs[:RING], [r[...] for r in refs[RING : 2 * RING]], refs[2 * RING :]
    p = at[0]
    for j in range(RING):
        own = lax.bitwise_xor(p, j)
        total = 0.0
        for i in range(RING):
            if i != j:
                there = lax.bitwise_xor(p, i)
                weight = jnp.exp(log_over(p, logs, lambda k: (k > own) & (k < there)))
                total += fronts[i][0].astype(f32) * jnp.where(there > own, weight, 0.0)
        outs[j][0] = total.astype(bf16)


def finish_kernel(n_heads, n_w, n_pieces, outer, share, at, *refs):
    locals_, refs = refs[:RING], refs[RING:]
    rings, refs = refs[:RING], refs[RING:]
    quarters, refs = refs[:RING], refs[RING:]
    logs, refs = [r[...] for r in refs[:RING]], refs[RING:]
    tops, refs = refs[:RING], refs[RING:]
    bottoms, refs = refs[:RING], refs[RING:]
    cums, refs = refs[:RING], refs[RING:]
    w, refs = refs[:n_pieces], refs[n_pieces:]
    x, acts, own, write, *tiles, total = refs
    g, p = pl.program_id(0), at[0]
    heads = n_heads // RING
    rows = own.shape[0]
    width = own.shape[1] // heads
    n = quarters[0].shape[0] - EXTRA
    source = lax.bitwise_xor(p, g)
    carried = quarters[0][:n].astype(f32)
    for j in range(1, RING):
        carried = jnp.where(source == j, quarters[j][:n].astype(f32), carried)

    @pl.when(g == 0)
    def _():
        write[...] = jnp.zeros_like(write)
        total[...] = jnp.zeros_like(total)

    for j in range(RING):
        col = group_of(cums[j][...], g, heads, 1)
        tail = spread(jnp.exp(col[rows - 1 : rows, :] - col), width)
        place = lax.bitwise_xor(p, j)
        weight = jnp.exp(log_over(p, logs, lambda k: k > place))
        grads = (carried * weight + rings[j][0].astype(f32)).astype(bf16)
        b = jnp.concatenate([tops[j][...], bottoms[j][...]], axis=0)
        out = mm(b, grads, NN) * tail + locals_[j][...].astype(f32)
        out = out.astype(acts.dtype)
        acts[j * rows : (j + 1) * rows, :] = out
        if j == 0:
            own[...] = out
            write[...] += mm((x[...].astype(f32) * tail).astype(bf16), grads, NT)
    n_rows, column = w[0].shape[0], 0
    for piece in w:
        total[:, column : column + piece.shape[0]] += mm(acts[...], piece[...], NT)
        column += piece.shape[0]

    @pl.when(g == pl.num_programs(0) - 1)
    def _():
        if len(tiles) == 1:
            for k in range(n_w):
                put_tile(tiles[0], lax.rem(at[1] + k, outer), total, k, n_rows)
        else:
            for tile in tiles:
                tile[...] = jnp.zeros_like(tile)
            for k in range(n_w):
                o = lax.rem(at[1] + k, outer)
                for tile, side in zip(tiles, (at[2], 1 - at[2])):

                    @pl.when(lax.div(o, share) == side)
                    def _():
                        put_tile(tile, lax.rem(o, share), total, k, n_rows)


def put_tile(tile, slot, total, k, n_rows):
    rows = total.shape[0] // RING
    for j in range(RING):
        part = total[j * rows : (j + 1) * rows, k * n_rows : (k + 1) * n_rows]
        tile[j, slot] = part.astype(tile.dtype)


def read_kernel(n_heads, at, *refs):
    tops, refs = refs[:RING], refs[RING:]
    bottoms, refs = refs[:RING], refs[RING:]
    cums, refs = refs[:RING], refs[RING:]
    parts, (carried, *outs) = refs[:RING], refs[RING:]
    logs = [log_of(part) for part in parts]
    p = at[0]
    heads = n_heads // RING
    half = tops[0].shape[0]
    n = carried.shape[0] - EXTRA
    width = carried.shape[1] // heads
    for j in range(RING):
        own = lax.bitwise_xor(p, j)
        total = carried[:n].astype(f32) * jnp.exp(log_over(p, logs, lambda k: k < own))
        for i in range(RING):
            if i != j:
                there = lax.bitwise_xor(p, i)
                weight = jnp.exp(log_over(p, logs, lambda k: (k < own) & (k > there)))
                total += parts[i][:n].astype(f32) * jnp.where(there < own, weight, 0.0)
        states = total.astype(bf16)
        decay = spread(jnp.exp(group_of(cums[j][...], p, heads, 1)), width)
        for i, dy in enumerate((tops[j], bottoms[j])):
            at_rows = slice(i * half, (i + 1) * half)
            scaled = (dy[...].astype(f32) * decay[at_rows]).astype(bf16)
            outs[j][at_rows] = mm(scaled, states, NT).astype(bf16)


def place_kernel(outer, share, at, *refs):
    blocks, late, out = refs[:RING], refs[RING:-1], refs[-1]
    p, z, side = at[0], at[1], at[2]
    width = out.shape[1] // (share * RING)
    last = lax.rem(z + outer - 1, outer)
    for slot in range(share):
        for j in range(RING):
            column = pl.multiple_of((slot * RING + lax.bitwise_xor(p, j)) * width, width)

            @pl.when(side * share + slot == last)
            def _():
                out[:, pl.ds(column, width)] = late[j][...]

            @pl.when(side * share + slot != last)
            def _():
                out[:, pl.ds(column, width)] = blocks[j][slot]


def call(kernel, name, grid, in_specs, out_specs, out_shape, scratch=(), after=(), flops=0):
    n_in, n_after = len(in_specs), len(after)

    def body(at, *refs):
        kernel(at, *refs[:n_in], *refs[n_in + n_after :])

    fn = pl.pallas_call(
        body,
        grid_spec=pltpu.PrefetchScalarGridSpec(
            num_scalar_prefetch=1,
            grid=grid,
            in_specs=list(in_specs) + [pl.BlockSpec(memory_space=pl.ANY)] * n_after,
            out_specs=out_specs,
            scratch_shapes=list(scratch),
        ),
        out_shape=out_shape,
        compiler_params=pltpu.CompilerParams(vmem_limit_bytes=56 * 2**20),
        cost_estimate=pl.CostEstimate(flops=flops, bytes_accessed=0, transcendentals=0),
        name=name,
    )
    return lambda *operands: fn(*operands, *after)


def local(x, dy, write_proj, read_proj, log_decay, w_in):
    rows, columns = x.shape
    half = rows // 2
    state_dim = write_proj.shape[1]
    n_heads = log_decay.shape[1]
    heads = n_heads // RING
    width = columns // n_heads
    part = heads * width
    w_rows = w_in.shape[0]
    n_seq, n_head = lax.axis_size("seq"), lax.axis_size("head")
    outer = n_seq // RING
    place = lax.axis_index("seq")
    side = lax.axis_index("head")
    p, z = place % RING, place // RING
    at = jnp.stack([p, z, side]).astype(jnp.int32)

    def swap(value, j):
        return lax.ppermute(value, "seq", [(s, s ^ j) for s in range(n_seq)])

    def along(value, d):
        return lax.ppermute(
            value, "seq", [(s, s + d * RING) for s in range(n_seq) if 0 <= s + d * RING < n_seq]
        )

    two = n_head == 2 and w_rows % LANES == 0 and outer == 4
    share = outer // n_head

    def turn(value):
        return lax.ppermute(value, "seq", [(s, (s - RING) % n_seq) for s in range(n_seq)])

    w_first = turn(w_in)

    def const(*shape):
        return pl.BlockSpec(shape, lambda g, q: (0,) * len(shape))

    by_group = pl.BlockSpec((rows, part), lambda g, q: (0, g))
    state_spec = pl.BlockSpec((1, state_dim, part), lambda g, q: (g, 0, 0))
    log_spec = pl.BlockSpec((1, part), lambda g, q: (0, g))
    cum_spec = const(rows, LANES)
    proj_spec = const(rows, state_dim)
    message_spec = const(state_dim + EXTRA, part)
    shape = jax.ShapeDtypeStruct
    state_shape = shape((RING, state_dim, part), bf16)
    log_shape = shape((1, columns), f32)
    cum_shape = shape((rows, LANES), f32)
    message_shape = shape((state_dim + EXTRA, part), bf16)
    cum_scratch, cum_t_scratch = pltpu.VMEM((rows, LANES), f32), pltpu.VMEM((LANES, rows), f32)

    log_in_spec = const(n_heads, rows)
    log_t = log_decay.T
    own_specs = [by_group, by_group, proj_spec, proj_spec, log_in_spec]
    part_spec = const(2 * state_dim + EXTRA, part)
    parts = call(
        functools.partial(edge_kernel, n_heads),
        "edges",
        (RING,),
        own_specs,
        [part_spec] * RING,
        [shape((2 * state_dim + EXTRA, part), bf16)] * RING,
        [cum_scratch],
    )(at, x, dy, write_proj, read_proj, log_t)

    write_local, read_local = call(
        functools.partial(lambda *refs: own_kernel(n_heads, *refs[1:])),
        "own_tokens",
        (RING,),
        own_specs,
        [proj_spec] * 2,
        [shape((rows, state_dim), f32)] * 2,
        [pltpu.VMEM((rows, rows), f32), cum_scratch, cum_t_scratch],
    )(at, x, dy, write_proj, read_proj, log_t)

    packed = call(
        functools.partial(lambda *refs: pack_kernel(n_heads, *refs[1:])),
        "pack",
        (1,),
        [const(rows, columns), proj_spec, proj_spec, log_in_spec],
        const(rows, columns + 3 * LANES),
        shape((rows, columns + 3 * LANES), bf16),
    )(at, dy, write_proj, read_proj, log_t)

    def halves(width, column):
        upper = pl.BlockSpec((half, width), lambda g, q: (0, column(g, q)))
        lower = pl.BlockSpec((half, width), lambda g, q: (1, column(g, q)))
        return [(upper, lower)] * (RING - 1) + [(upper, upper)]

    half_specs = halves(part, lambda g, q: g)
    mine_specs = halves(part, lambda g, q: q[0])
    tile_specs = [halves(LANES, lambda g, q, i=i: columns // LANES + i) for i in range(3)]

    def block(j, top, bottom, after=()):
        return call(
            functools.partial(lambda *refs: block_kernel(n_heads, *refs[1:])),
            "tokens",
            (RING,),
            [*half_specs[j]] + [spec for specs in tile_specs for spec in specs[j]],
            [by_group, state_spec, log_spec, cum_spec],
            [shape((rows, columns), bf16), state_shape, log_shape, cum_shape],
            [cum_t_scratch],
            after,
            flops=2 * rows * rows * columns * 16 if j else 0,
        )(at, top, bottom, *([top, bottom] * 3))

    results = [block(0, packed, packed)]
    from_x, from_y = swap(packed, 1), swap(packed, 2)
    results.append(block(1, from_x, from_x, after=[w_first, read_local]))
    results.append(block(2, from_y, from_y))
    from_x, from_y, parts = lax.optimization_barrier((from_x, from_y, parts))
    parts = [parts[0]] + [swap(parts[j], j) for j in range(1, RING)]
    logs = [v[2] for v in results]
    from_x, from_y, logs, parts = lax.optimization_barrier((from_x, from_y, logs, parts))
    blocks = [(packed, packed), (from_x, from_x), (from_y, from_y)]
    blocks.append((swap(from_x[:half], 2), swap(from_y[half:], 1)))
    results.append(block(RING - 1, *blocks[-1]))
    logs.append(results[-1][2])
    local_acts, fronts, _, cums = zip(*results)

    def combine():
        return call(
            combine_kernel,
            "messages",
            (1,),
            [part_spec] * RING,
            [message_spec] * 2,
            [message_shape] * 2,
        )(at, *parts)

    def merge(*pairs, after=()):
        return call(
            lambda q, *refs: merge_kernel(*refs),
            "merge",
            (1,),
            [message_spec] * 4,
            [message_spec] * 2,
            [message_shape] * 2,
            after=after,
        )(at, *pairs)

    w_pieces = [w_in, w_first]
    while len(w_pieces) < outer - 1:
        w_pieces.append(turn(w_pieces[-1]))
    state_span, grad_span = combine()
    d = 1
    while d < outer:
        state_got, grad_got = along(state_span, d), along(grad_span, -d)
        if d == 1:
            state_part, grad_part = state_got, grad_got
        else:
            after = [logs[-1]] if 2 * d >= outer else []
            state_part, grad_part = merge(
                state_part, state_got, grad_part, grad_got, after=after
            )
        if 2 * d < outer:
            state_span, grad_span = merge(state_span, state_got, grad_span, grad_got)
        d *= 2
    grad_part, w_last = lax.optimization_barrier((grad_part, w_pieces[-1]))
    w_last = turn(w_last)
    if not two:
        w_pieces.append(w_last)
    grad_parts = [grad_part] + [swap(grad_part, j) for j in range(1, RING)]

    ring_grads = call(
        ring_kernel,
        "ring_grads",
        (RING,),
        [state_spec] * RING + [log_spec] * RING,
        [state_spec] * RING,
        [state_shape] * RING,
    )(at, *fronts, *logs)

    n_w = outer - 1 if two else outer
    tall = pl.BlockSpec((RING * rows, part), lambda g, q: (0, g))
    tile_shapes = [(RING, outer, rows, w_rows)]
    if two:
        tile_shapes = [(RING, share, rows, w_rows)] * 2
    w_total = sum(v.shape[0] for v in w_pieces)
    acts, act_grad, write_carry, *tiles = call(
        functools.partial(finish_kernel, n_heads, n_w, len(w_pieces), outer, share),
        "finish",
        (RING,),
        [by_group] * RING
        + [state_spec] * RING
        + [message_spec] * RING
        + [log_spec] * RING
        + [spec[0] for spec in tile_specs[0]]
        + [spec[1] for spec in tile_specs[0]]
        + [cum_spec] * RING
        + [pl.BlockSpec((v.shape[0], part), lambda g, q: (0, g)) for v in w_pieces]
        + [by_group],
        [tall, by_group, proj_spec] + [const(*v) for v in tile_shapes],
        [
            shape((RING * rows, columns), bf16),
            shape((rows, columns), bf16),
            shape((rows, state_dim), f32),
        ]
        + [shape(v, bf16) for v in tile_shapes],
        [pltpu.VMEM((RING * rows, w_total), f32)],
        flops=2 * RING * rows * columns * w_total,
    )(
        at,
        *local_acts,
        *ring_grads,
        *grad_parts,
        *logs,
        *[top for top, _ in blocks],
        *[bottom for _, bottom in blocks],
        *cums,
        *w_pieces,
        x,
    )

    def to_owners(tile):
        return [tile[0]] + [swap(tile[j], j) for j in range(1, RING)]

    read_parts = call(
        functools.partial(read_kernel, n_heads),
        "read_carry",
        (1,),
        [spec[0] for spec in mine_specs]
        + [spec[1] for spec in mine_specs]
        + [cum_spec] * RING + [part_spec] * RING + [message_spec],
        [proj_spec] * RING,
        [shape((rows, state_dim), bf16)] * RING,
        after=[write_carry],
    )(
        at,
        *[top for top, _ in blocks],
        *[bottom for _, bottom in blocks],
        *cums,
        *parts,
        state_part,
    )
    read_got = [swap(read_parts[j], j) for j in range(1, RING)]
    if two:
        mine, theirs = tiles
        got = lax.ppermute(theirs, "head", [(0, 1), (1, 0)])
        early = (mine.astype(f32) + got.astype(f32)).astype(bf16)
        early, read_own, w_last = lax.optimization_barrier((early, read_parts[0], w_last))
        late = mm(acts, w_last, NT).astype(bf16)

        def owner(s):
            return (s // RING + outer - 1) % outer // share

        both_axes = ("seq", "head")
        got = lax.ppermute(
            late, both_axes, [(2 * s + 1 - owner(s), 2 * s + owner(s)) for s in range(n_seq)]
        )
        early_sent = to_owners(early)
        got, read_got, early_sent = lax.optimization_barrier((got, read_got, early_sent))
        late = (late.astype(f32) + got.astype(f32)).astype(bf16).reshape(RING, rows, w_rows)
        late = [late[0]] + [
            lax.ppermute(
                late[j],
                both_axes,
                [(2 * s + owner(s), 2 * (s ^ j) + owner(s)) for s in range(n_seq)],
            )
            for j in range(1, RING)
        ]
        input_grad = pl.pallas_call(
            functools.partial(place_kernel, outer, share),
            in_specs=[pl.BlockSpec(memory_space=pltpu.SMEM)]
            + [pl.BlockSpec(memory_space=pltpu.VMEM)] * (2 * RING),
            out_specs=pl.BlockSpec(memory_space=pltpu.VMEM),
            out_shape=shape((rows, share * RING * w_rows), bf16),
            compiler_params=pltpu.CompilerParams(vmem_limit_bytes=32 * 2**20),
            name="place",
        )(at, *early_sent, *late)
    else:
        summed = lax.psum_scatter(tiles[0], "head", scatter_dimension=1, tiled=True)
        pieces = jnp.take(jnp.stack(to_owners(summed)), p ^ jnp.arange(RING), axis=0)
        input_grad = pieces.transpose(2, 1, 0, 3).reshape(rows, share * RING * w_rows)
    read_carry = read_parts[0].astype(f32) + sum(v.astype(f32) for v in read_got)
    both = jnp.stack([write_local + write_carry, read_local + read_carry])
    if n_head == 2:
        both = both + lax.ppermute(both, "head", [(0, 1), (1, 0)])
    else:
        both = lax.psum(both, "head")
    return (input_grad, act_grad, both[0], both[1])


def solution(mesh):
    return jax.shard_map(
        local,
        mesh=mesh,
        in_specs=(
            P("seq", "head"),
            P("seq", "head"),
            P("seq", None),
            P("seq", None),
            P("seq", "head"),
            P("seq", "head"),
        ),
        out_specs=(P("seq", "head"), P("seq", "head"), P("seq", None), P("seq", None)),
        check_vma=False,
    )
```

profile of v0, /device:TPU:1, one launch (start us, length us, event | category | flops | bytes accessed | tf_op | source)
XLA Modules:
  0.0 229.6 jit_solution(3142989330574753512)
XLA Ops:
  1.3 4.0 %pack.1.refs_0_.refs_1_.refs_2_.refs_3_.refs_4_.refs_5_.refs_6_.refs_7_.refs_16_.refs_20_ = bf16[256,4480]{1,0:T(8,128)(2,1)} custom-call(s32[3]{0:T(128)} %pad_add_fusion.at, bf16[256,4096]{1,0:T(8,128)(2,1)} %refs_1_.5, bf16[256,128]{1,0:T(8,128)(2,1)} %refs_2_.5, bf16[256,128]{1,0:T(8,128)(2,1)} %refs_3_.3, f32[32,256]{1,0:T(8,128)} %bitcast.22), custom_call_target="tpu_custom_call" | custom-call | tf_op jit(solution)/shard_map/pack/pallas_call | solution.py:381
  8.5 3.3 %collective-permute-start.1 = (bf16[256,4096]{1,0:T(8,128)(2,1)S(1)}, bf16[256,4096]{1,0:T(8,128)(2,1)}, u32[]{:S(2)}, u32[]{:S(2)}) collective-permute-start(bf16[256,4096]{1,0:T(8,128)(2,1)S(1)} %copy-done.10), channel_id=1, source_target_pairs={{0,24},{2,26},{4,28},{6,30},{8,0},{10,2},{12,4},{14,6},{16,8},{18,... | collective-permute-start | bytes 6291464 | tf_op jit(solution)/shard_map/ppermute | solution.py:412
  11.8 8.2 %own_tokens.1 = (f32[256,128]{1,0:T(8,128)}, f32[256,128]{1,0:T(8,128)}) custom-call(s32[3]{0:T(128)} %pad_add_fusion.at, bf16[256,4096]{1,0:T(8,128)(2,1)} %refs_31_.1, bf16[256,4096]{1,0:T(8,128)(2,1)} %refs_1_.5, bf16[256,128]{1,0:T(8,128)(2,1)} %refs_2_.5, bf16[256,128]{1,0:T(8,128)(2,1)} %refs_3_.3, f32[32,256]{1,0:T(8,128)} %bitcast.23), custom_call_target="tpu_custom_call" | custom-call | tf_op jit(solution)/shard_map/own_tokens/pallas_call | solution.py:381
  20.0 8.1 %edges.1 = (bf16[272,1024]{1,0:T(8,128)(2,1)}, bf16[272,1024]{1,0:T(8,128)(2,1)}, bf16[272,1024]{1,0:T(8,128)(2,1)}, bf16[272,1024]{1,0:T(8,128)(2,1)}) custom-call(s32[3]{0:T(128)} %pad_add_fusion.at, bf16[256,4096]{1,0:T(8,128)(2,1)} %refs_31_.1, bf16[256,4096]{1,0:T(8,128)(2,1)} %refs_1_.5, bf16[256,128]{1,0:T(8,128)(2,1)} %refs_2_.5, ...), custom_call_target="tpu_custom_call" | custom-call | tf_op jit(solution)/shard_map/edges/pallas_call | solution.py:381
  28.2 8.1 %tokens.4 = (bf16[256,4096]{1,0:T(8,128)(2,1)}, bf16[4,128,1024]{2,1,0:T(8,128)(2,1)}, f32[1,4096]{1,0:T(1,128)}, f32[256,128]{1,0:T(8,128)}) custom-call(s32[3]{0:T(128)} %pad_add_fusion.at, bf16[256,4480]{1,0:T(8,128)(2,1)} %pack.1.refs_0_.refs_1_.refs_2_.refs_3_.refs_4_.refs_5_.refs_6_.refs_7_.refs_16_.refs_20_, ...), custom_call_target="tpu_custom_call" | custom-call | tf_op jit(solution)/shard_map/tokens/pallas_call | solution.py:381
  36.2 19.3 %collective-permute-done.1.refs_8_.refs_29_ = bf16[256,4096]{1,0:T(8,128)(2,1)} collective-permute-done((bf16[256,4096]{1,0:T(8,128)(2,1)S(1)}, bf16[256,4096]{1,0:T(8,128)(2,1)}, u32[]{:S(2)}, u32[]{:S(2)}) %collective-permute-start.1) | collective-permute-done | bytes 2097184 | tf_op jit(solution)/shard_map/ppermute | solution.py:412
  55.5 4.1 %collective-permute-start.12 = (bf16[256,4096]{1,0:T(8,128)(2,1)}, bf16[256,4096]{1,0:T(8,128)(2,1)}, u32[]{:S(2)}, u32[]{:S(2)}) collective-permute-start(bf16[256,4096]{1,0:T(8,128)(2,1)} %collective-permute-done.1.refs_8_.refs_29_), channel_id=1, source_target_pairs={{0,24},{2,26},{4,28},{6,30},{8,0},{10,2},{12,4},{14,6},{16,8},{18,... | collective-permute-start | bytes 6291464 | tf_op jit(solution)/shard_map/ppermute | solution.py:412
  60.2 2.2 collective-permute-start.5
  62.4 8.0 %tokens.6 = (bf16[256,4096]{1,0:T(8,128)(2,1)}, bf16[4,128,1024]{2,1,0:T(8,128)(2,1)}, f32[1,4096]{1,0:T(1,128)}, f32[256,128]{1,0:T(8,128)}) custom-call(s32[3]{0:T(128)} %pad_add_fusion.at, bf16[256,4480]{1,0:T(8,128)(2,1)} %copy-done.1, bf16[256,4480]{1,0:T(8,128)(2,1)} %copy-done.1, bf16[256,4480]{1,0:T(8,128)(2,1)} %copy-done.1, ...), custom_call_target="tpu_custom_call" | custom-call | flops 8589934592 | tf_op jit(solution)/shard_map/tokens/pallas_call | solution.py:381
  70.4 8.1 %tokens.5 = (bf16[256,4096]{1,0:T(8,128)(2,1)}, bf16[4,128,1024]{2,1,0:T(8,128)(2,1)}, f32[1,4096]{1,0:T(1,128)}, f32[256,128]{1,0:T(8,128)}) custom-call(s32[3]{0:T(128)} %pad_add_fusion.at, bf16[256,4480]{1,0:T(8,128)(2,1)} %copy-done.3, bf16[256,4480]{1,0:T(8,128)(2,1)} %copy-done.3, bf16[256,4480]{1,0:T(8,128)(2,1)} %copy-done.3, ...), custom_call_target="tpu_custom_call" | custom-call | flops 8589934592 | tf_op jit(solution)/shard_map/tokens/pallas_call | solution.py:381
  78.5 5.0 %collective-permute-done.5.refs_3_.refs_15_ = bf16[272,1024]{1,0:T(8,128)(2,1)S(1)} collective-permute-done((bf16[272,1024]{1,0:T(8,128)(2,1)S(1)}, bf16[272,1024]{1,0:T(8,128)(2,1)S(1)}, u32[]{:S(2)}, u32[]{:S(2)}) %collective-permute-start.5) | collective-permute-done | bytes 557088 | tf_op jit(solution)/shard_map/ppermute | solution.py:401
  85.8 3.4 %messages.1 = (bf16[144,1024]{1,0:T(8,128)(2,1)}, bf16[144,1024]{1,0:T(8,128)(2,1)}) custom-call(s32[3]{0:T(128)} %pad_add_fusion.at, bf16[272,1024]{1,0:T(8,128)(2,1)} %get-tuple-element.104.refs_0_.refs_12_, bf16[272,1024]{1,0:T(8,128)(2,1)} %copy-done.7, bf16[272,1024]{1,0:T(8,128)(2,1)} %copy-done.8, bf16[272,1024]{1,0:T(8,128)(2,1)} %copy-done.9), custom_call_target="tpu_custom_call" | custom-call | tf_op jit(solution)/shard_map/messages/pallas_call | solution.py:381
  89.2 2.9 %collective-permute-start.8 = (bf16[144,1024]{1,0:T(8,128)(2,1)}, bf16[144,1024]{1,0:T(8,128)(2,1)S(1)}, u32[]{:S(2)}, u32[]{:S(2)}) collective-permute-start(bf16[144,1024]{1,0:T(8,128)(2,1)} %get-tuple-element.108.refs_0_), channel_id=1, source_target_pairs={{0,8},{2,10},{4,12},{6,14},{8,16},{10,18},{12,20},{14,22},{16,24},... | collective-permute-start | bytes 884744 | tf_op jit(solution)/shard_map/ppermute | solution.py:404
  93.5 15.6 %collective-permute-done.8.refs_1_.refs_0_ = bf16[144,1024]{1,0:T(8,128)(2,1)S(1)} collective-permute-done((bf16[144,1024]{1,0:T(8,128)(2,1)}, bf16[144,1024]{1,0:T(8,128)(2,1)S(1)}, u32[]{:S(2)}, u32[]{:S(2)}) %collective-permute-start.8) | collective-permute-done | bytes 294944 | tf_op jit(solution)/shard_map/ppermute | solution.py:404
  110.5 2.9 %merge.2 = (bf16[144,1024]{1,0:T(8,128)(2,1)}, bf16[144,1024]{1,0:T(8,128)(2,1)}) custom-call(s32[3]{0:T(128)} %pad_add_fusion.at, bf16[144,1024]{1,0:T(8,128)(2,1)} %get-tuple-element.108.refs_0_, bf16[144,1024]{1,0:T(8,128)(2,1)} %copy-done.11, bf16[144,1024]{1,0:T(8,128)(2,1)} %get-tuple-element.109.refs_2_, bf16[144,1024]{1,0:T(8,128)(2,1)} %copy-done.12), custom_call_target="tpu_custom_call" | custom-call | tf_op jit(solution)/shard_map/merge/pallas_call | solution.py:381
  113.4 7.5 %collective-permute-start.10 = (bf16[144,1024]{1,0:T(8,128)(2,1)}, bf16[144,1024]{1,0:T(8,128)(2,1)S(1)}, u32[]{:S(2)}, u32[]{:S(2)}) collective-permute-start(bf16[144,1024]{1,0:T(8,128)(2,1)} %get-tuple-element.110), channel_id=1, source_target_pairs={{0,16},{2,18},{4,20},{6,22},{8,24},{10,26},{12,28},{14,30},{1,17},... | collective-permute-start | bytes 884744 | tf_op jit(solution)/shard_map/ppermute | solution.py:404
  124.2 8.0 %tokens.7 = (bf16[256,4096]{1,0:T(8,128)(2,1)}, bf16[4,128,1024]{2,1,0:T(8,128)(2,1)}, f32[1,4096]{1,0:T(1,128)}, f32[256,128]{1,0:T(8,128)}) custom-call(s32[3]{0:T(128)} %pad_add_fusion.at, bf16[128,4480]{1,0:T(8,128)(2,1)} %copy-done.6, bf16[128,4480]{1,0:T(8,128)(2,1)} %copy-done.5, bf16[128,4480]{1,0:T(8,128)(2,1)} %copy-done.6, ...), custom_call_target="tpu_custom_call" | custom-call | flops 8589934592 | tf_op jit(solution)/shard_map/tokens/pallas_call | solution.py:381
  132.2 6.0 %collective-permute-done.11.refs_3_ = bf16[144,1024]{1,0:T(8,128)(2,1)S(1)} collective-permute-done((bf16[144,1024]{1,0:T(8,128)(2,1)}, bf16[144,1024]{1,0:T(8,128)(2,1)S(1)}, u32[]{:S(2)}, u32[]{:S(2)}) %collective-permute-start.11) | collective-permute-done | bytes 294944 | tf_op jit(solution)/shard_map/ppermute | solution.py:404
  138.9 2.8 %merge.3 = (bf16[144,1024]{1,0:T(8,128)(2,1)}, bf16[144,1024]{1,0:T(8,128)(2,1)}) custom-call(s32[3]{0:T(128)} %pad_add_fusion.at, bf16[144,1024]{1,0:T(8,128)(2,1)} %copy-done.11, bf16[144,1024]{1,0:T(8,128)(2,1)} %copy-done.18, bf16[144,1024]{1,0:T(8,128)(2,1)} %copy-done.12, bf16[144,1024]{1,0:T(8,128)(2,1)} %copy-done.19, ...), custom_call_target="tpu_custom_call" | custom-call | tf_op jit(solution)/shard_map/merge/pallas_call | solution.py:381
  144.4 6.1 %ring_grads.1 = (bf16[4,128,1024]{2,1,0:T(8,128)(2,1)}, bf16[4,128,1024]{2,1,0:T(8,128)(2,1)}, bf16[4,128,1024]{2,1,0:T(8,128)(2,1)}, bf16[4,128,1024]{2,1,0:T(8,128)(2,1)}) custom-call(s32[3]{0:T(128)} %pad_add_fusion.at, bf16[4,128,1024]{2,1,0:T(8,128)(2,1)} %get-tuple-element.92.refs_0_, bf16[4,128,1024]{2,1,0:T(8,128)(2,1)} %get-tuple-element.93.refs_1_, ...), custom_call_target="tpu_custom_call" | custom-call | tf_op jit(solution)/shard_map/ring_grads/pallas_call | solution.py:381
  150.5 6.0 %collective-permute-done.14.refs_10_ = bf16[144,1024]{1,0:T(8,128)(2,1)S(1)} collective-permute-done((bf16[144,1024]{1,0:T(8,128)(2,1)}, bf16[144,1024]{1,0:T(8,128)(2,1)S(1)}, u32[]{:S(2)}, u32[]{:S(2)}) %collective-permute-start.14) | collective-permute-done | bytes 294944 | tf_op jit(solution)/shard_map/ppermute | solution.py:401
  157.3 21.1 %finish.1 = (bf16[1024,4096]{1,0:T(8,128)(2,1)}, bf16[256,4096]{1,0:T(8,128)(2,1)}, f32[256,128]{1,0:T(8,128)}, bf16[4,2,256,256]{3,2,1,0:T(8,128)(2,1)}, bf16[4,2,256,256]{3,2,1,0:T(8,128)(2,1)}) custom-call(s32[3]{0:T(128)} %pad_add_fusion.at, bf16[256,4096]{1,0:T(8,128)(2,1)} %get-tuple-element.72.refs_0_, bf16[256,4096]{1,0:T(8,128)(2,1)} %get-tuple-element.74.refs_1_, ...), custom_call_target="tpu_custom_call" | custom-call | flops 6442450944 | tf_op jit(solution)/shard_map/finish/pallas_call | solution.py:381
  179.8 6.4 %read_carry.1 = (bf16[256,128]{1,0:T(8,128)(2,1)}, bf16[256,128]{1,0:T(8,128)(2,1)}, bf16[256,128]{1,0:T(8,128)(2,1)}, bf16[256,128]{1,0:T(8,128)(2,1)}) custom-call(s32[3]{0:T(128)} %pad_add_fusion.at, bf16[256,4480]{1,0:T(8,128)(2,1)} %pack.1.refs_0_.refs_1_.refs_2_.refs_3_.refs_4_.refs_5_.refs_6_.refs_7_.refs_16_.refs_20_, bf16[256,4480]{1,0:T(8,128)(2,1)} %copy-done.3, ...), custom_call_target="tpu_custom_call" | custom-call | tf_op jit(solution)/shard_map/read_carry/pallas_call | solution.py:381
  186.5 2.9 %collective-permute-done.17 = bf16[256,4096]{1,0:T(8,128)(2,1)S(1)} collective-permute-done((bf16[256,4096]{1,0:T(8,128)(2,1)}, bf16[256,4096]{1,0:T(8,128)(2,1)S(1)}, u32[]{:S(2)}, u32[]{:S(2)}) %collective-permute-start.17) | collective-permute-done | bytes 2097184 | tf_op jit(solution)/shard_map/ppermute | solution.py:412
  189.5 5.8 %convolution_convert_fusion = bf16[1024,256]{1,0:T(8,128)(2,1)S(1)} fusion(bf16[1024,4096]{1,0:T(8,128)(2,1)} %get-tuple-element.118, bf16[256,4096]{1,0:T(8,128)(2,1)S(1)} %collective-permute-done.17), kind=kOutput, calls=%fused_computation.1 | convolution fusion | flops 2147745792 | bytes 11010048 | tf_op jit(solution)/shard_map/dot_general | solution.py:20
  197.3 2.3 collective-permute-start.24
  200.1 2.2 collective-permute-start.21
  202.3 8.5 %collective-permute-done.21 = bf16[256,128]{1,0:T(8,128)(2,1)S(1)} collective-permute-done((bf16[256,128]{1,0:T(8,128)(2,1)S(1)}, bf16[256,128]{1,0:T(8,128)(2,1)S(1)}, u32[]{:S(2)}, u32[]{:S(2)}) %collective-permute-start.21) | collective-permute-done | bytes 65568 | tf_op jit(solution)/shard_map/ppermute | solution.py:401
  212.2 2.8 %collective-permute-start.28 = (f32[2,256,128]{2,1,0:T(8,128)S(1)}, f32[2,256,128]{2,1,0:T(8,128)S(1)}, u32[]{:S(2)}, u32[]{:S(2)}) collective-permute-start(f32[2,256,128]{2,1,0:T(8,128)S(1)} %pad_maximum_fusion), channel_id=1, source_target_pairs={{0,1},{1,0},{2,3},{3,2},{4,5},{5,4},{6,7},{7,6},{8,9},{9,8},{10,11... | collective-permute-start | bytes 786440 | tf_op jit(solution)/shard_map/ppermute | solution.py:658
  215.1 4.2 %collective-permute-start.27 = (bf16[256,256]{1,0:T(8,128)(2,1)S(1)}, bf16[256,256]{1,0:T(8,128)(2,1)S(1)}, u32[]{:S(2)}, u32[]{:S(2)}) collective-permute-start(bf16[256,256]{1,0:T(8,128)(2,1)S(1)} %get-tuple-element.144), channel_id=1, source_target_pairs={{1,7},{3,5},{5,3},{7,1},{8,14},{10,12},{12,10},{14,8},{16,22},{18,... | collective-permute-start | bytes 393224 | tf_op jit(solution)/shard_map/ppermute | solution.py:635
  221.4 2.1 collective-permute-start.25
  225.0 2.1 collective-permute-done.25.refs_5_
  (109 shorter events, 28.6 us)
Async XLA Ops:
  5.2 54.4 %collective-permute-start.2 = (bf16[256,4480]{1,0:T(8,128)(2,1)}, bf16[256,4480]{1,0:T(8,128)(2,1)S(1)}, u32[]{:S(2)}, u32[]{:S(2)}) collective-permute-start(bf16[256,4480]{1,0:T(8,128)(2,1)} %pack.1.refs_0_.refs_1_.refs_2_.refs_3_.refs_4_.refs_5_.refs_6_.refs_7_.refs_16_.refs_20_), channel_id=1, source_target_pairs={{0,4},{2,6},{4,0},{6,2},{8,12},{10,14},{12,8},{14,10},{16,20},{18,... | collective-permute-start | bytes 6881288 | tf_op jit(solution)/shard_map/ppermute | solution.py:401
  7.3 52.3 %collective-permute-start = (bf16[256,4480]{1,0:T(8,128)(2,1)}, bf16[256,4480]{1,0:T(8,128)(2,1)S(1)}, u32[]{:S(2)}, u32[]{:S(2)}) collective-permute-start(bf16[256,4480]{1,0:T(8,128)(2,1)} %pack.1.refs_0_.refs_1_.refs_2_.refs_3_.refs_4_.refs_5_.refs_6_.refs_7_.refs_16_.refs_20_), channel_id=1, source_target_pairs={{0,2},{2,0},{4,6},{6,4},{8,10},{10,8},{12,14},{14,12},{16,18},{18,... | collective-permute-start | bytes 6881288 | tf_op jit(solution)/shard_map/ppermute | solution.py:401
  8.5 47.0 %collective-permute-start.1 = (bf16[256,4096]{1,0:T(8,128)(2,1)S(1)}, bf16[256,4096]{1,0:T(8,128)(2,1)}, u32[]{:S(2)}, u32[]{:S(2)}) collective-permute-start(bf16[256,4096]{1,0:T(8,128)(2,1)S(1)} %copy-done.10), channel_id=1, source_target_pairs={{0,24},{2,26},{4,28},{6,30},{8,0},{10,2},{12,4},{14,6},{16,8},{18,... | collective-permute-start | bytes 6291464 | tf_op jit(solution)/shard_map/ppermute | solution.py:412
  28.1 31.8 %copy-start.24 = (bf16[272,1024]{1,0:T(8,128)(2,1)S(1)}, bf16[272,1024]{1,0:T(8,128)(2,1)}, u32[]{:S(2)}) copy-start(bf16[272,1024]{1,0:T(8,128)(2,1)} %get-tuple-element.87) | copy-start | bytes 1671172
  28.1 32.0 %copy-start.23 = (bf16[272,1024]{1,0:T(8,128)(2,1)S(1)}, bf16[272,1024]{1,0:T(8,128)(2,1)}, u32[]{:S(2)}) copy-start(bf16[272,1024]{1,0:T(8,128)(2,1)} %get-tuple-element.88) | copy-start | bytes 1671172
  55.5 86.2 %collective-permute-start.12 = (bf16[256,4096]{1,0:T(8,128)(2,1)}, bf16[256,4096]{1,0:T(8,128)(2,1)}, u32[]{:S(2)}, u32[]{:S(2)}) collective-permute-start(bf16[256,4096]{1,0:T(8,128)(2,1)} %collective-permute-done.1.refs_8_.refs_29_), channel_id=1, source_target_pairs={{0,24},{2,26},{4,28},{6,30},{8,0},{10,2},{12,4},{14,6},{16,8},{18,... | collective-permute-start | bytes 6291464 | tf_op jit(solution)/shard_map/ppermute | solution.py:412
  59.6 18.8 %collective-permute-start.3 = (bf16[272,1024]{1,0:T(8,128)(2,1)}, bf16[272,1024]{1,0:T(8,128)(2,1)S(1)}, u32[]{:S(2)}, u32[]{:S(2)}) collective-permute-start(bf16[272,1024]{1,0:T(8,128)(2,1)} %get-tuple-element.86), channel_id=1, source_target_pairs={{0,2},{2,0},{4,6},{6,4},{8,10},{10,8},{12,14},{14,12},{16,18},{18,... | collective-permute-start | bytes 1671176 | tf_op jit(solution)/shard_map/ppermute | solution.py:401
  60.0 18.5 %collective-permute-start.4 = (bf16[272,1024]{1,0:T(8,128)(2,1)S(1)}, bf16[272,1024]{1,0:T(8,128)(2,1)S(1)}, u32[]{:S(2)}, u32[]{:S(2)}) collective-permute-start(bf16[272,1024]{1,0:T(8,128)(2,1)S(1)} %copy-done.24), channel_id=1, source_target_pairs={{0,4},{2,6},{4,0},{6,2},{8,12},{10,14},{12,8},{14,10},{16,20},{18,... | collective-permute-start | bytes 1671176 | tf_op jit(solution)/shard_map/ppermute | solution.py:401
  60.2 23.3 %collective-permute-start.5 = (bf16[272,1024]{1,0:T(8,128)(2,1)S(1)}, bf16[272,1024]{1,0:T(8,128)(2,1)S(1)}, u32[]{:S(2)}, u32[]{:S(2)}) collective-permute-start(bf16[272,1024]{1,0:T(8,128)(2,1)S(1)} %copy-done.23), channel_id=1, source_target_pairs={{0,6},{2,4},{4,2},{6,0},{8,14},{10,12},{12,10},{14,8},{16,22},{18,... | collective-permute-start | bytes 1671176 | tf_op jit(solution)/shard_map/ppermute | solution.py:401
  84.3 37.8 %collective-permute-start.7 = (bf16[128,4480]{1,0:T(8,128)(2,1)S(1)}, bf16[128,4480]{1,0:T(8,128)(2,1)S(1)}, u32[]{:S(2)}, u32[]{:S(2)}) collective-permute-start(bf16[128,4480]{1,0:T(8,128)(2,1)S(1)} %slice.41), channel_id=1, source_target_pairs={{0,2},{2,0},{4,6},{6,4},{8,10},{10,8},{12,14},{14,12},{16,18},{18,... | collective-permute-start | bytes 3440648 | tf_op jit(solution)/shard_map/ppermute | solution.py:401
  84.6 37.5 %collective-permute-start.6 = (bf16[128,4480]{1,0:T(8,128)(2,1)S(1)}, bf16[128,4480]{1,0:T(8,128)(2,1)S(1)}, u32[]{:S(2)}, u32[]{:S(2)}) collective-permute-start(bf16[128,4480]{1,0:T(8,128)(2,1)S(1)} %slice.40), channel_id=1, source_target_pairs={{0,4},{2,6},{4,0},{6,2},{8,12},{10,14},{12,8},{14,10},{16,20},{18,... | collective-permute-start | bytes 3440648 | tf_op jit(solution)/shard_map/ppermute | solution.py:401
  89.2 19.8 %collective-permute-start.8 = (bf16[144,1024]{1,0:T(8,128)(2,1)}, bf16[144,1024]{1,0:T(8,128)(2,1)S(1)}, u32[]{:S(2)}, u32[]{:S(2)}) collective-permute-start(bf16[144,1024]{1,0:T(8,128)(2,1)} %get-tuple-element.108.refs_0_), channel_id=1, source_target_pairs={{0,8},{2,10},{4,12},{6,14},{8,16},{10,18},{12,20},{14,22},{16,24},... | collective-permute-start | bytes 884744 | tf_op jit(solution)/shard_map/ppermute | solution.py:404
  92.2 16.9 %collective-permute-start.9 = (bf16[144,1024]{1,0:T(8,128)(2,1)}, bf16[144,1024]{1,0:T(8,128)(2,1)S(1)}, u32[]{:S(2)}, u32[]{:S(2)}) collective-permute-start(bf16[144,1024]{1,0:T(8,128)(2,1)} %get-tuple-element.109.refs_2_), channel_id=1, source_target_pairs={{8,0},{10,2},{12,4},{14,6},{16,8},{18,10},{20,12},{22,14},{24,16},... | collective-permute-start | bytes 884744 | tf_op jit(solution)/shard_map/ppermute | solution.py:404
  113.4 18.8 %collective-permute-start.10 = (bf16[144,1024]{1,0:T(8,128)(2,1)}, bf16[144,1024]{1,0:T(8,128)(2,1)S(1)}, u32[]{:S(2)}, u32[]{:S(2)}) collective-permute-start(bf16[144,1024]{1,0:T(8,128)(2,1)} %get-tuple-element.110), channel_id=1, source_target_pairs={{0,16},{2,18},{4,20},{6,22},{8,24},{10,26},{12,28},{14,30},{1,17},... | collective-permute-start | bytes 884744 | tf_op jit(solution)/shard_map/ppermute | solution.py:404
  120.8 17.3 %collective-permute-start.11 = (bf16[144,1024]{1,0:T(8,128)(2,1)}, bf16[144,1024]{1,0:T(8,128)(2,1)S(1)}, u32[]{:S(2)}, u32[]{:S(2)}) collective-permute-start(bf16[144,1024]{1,0:T(8,128)(2,1)} %get-tuple-element.111), channel_id=1, source_target_pairs={{16,0},{18,2},{20,4},{22,6},{24,8},{26,10},{28,12},{30,14},{17,1},... | collective-permute-start | bytes 884744 | tf_op jit(solution)/shard_map/ppermute | solution.py:404
  141.7 8.8 %collective-permute-start.15 = (bf16[144,1024]{1,0:T(8,128)(2,1)}, bf16[144,1024]{1,0:T(8,128)(2,1)S(1)}, u32[]{:S(2)}, u32[]{:S(2)}) collective-permute-start(bf16[144,1024]{1,0:T(8,128)(2,1)} %get-tuple-element.113.refs_8_), channel_id=1, source_target_pairs={{0,6},{2,4},{4,2},{6,0},{8,14},{10,12},{12,10},{14,8},{16,22},{18,... | collective-permute-start | bytes 884744 | tf_op jit(solution)/shard_map/ppermute | solution.py:401
  141.9 14.7 %collective-permute-start.14 = (bf16[144,1024]{1,0:T(8,128)(2,1)}, bf16[144,1024]{1,0:T(8,128)(2,1)S(1)}, u32[]{:S(2)}, u32[]{:S(2)}) collective-permute-start(bf16[144,1024]{1,0:T(8,128)(2,1)} %get-tuple-element.113.refs_8_), channel_id=1, source_target_pairs={{0,4},{2,6},{4,0},{6,2},{8,12},{10,14},{12,8},{14,10},{16,20},{18,... | collective-permute-start | bytes 884744 | tf_op jit(solution)/shard_map/ppermute | solution.py:401
  143.1 13.4 %collective-permute-start.13 = (bf16[144,1024]{1,0:T(8,128)(2,1)}, bf16[144,1024]{1,0:T(8,128)(2,1)S(1)}, u32[]{:S(2)}, u32[]{:S(2)}) collective-permute-start(bf16[144,1024]{1,0:T(8,128)(2,1)} %get-tuple-element.113.refs_8_), channel_id=1, source_target_pairs={{0,2},{2,0},{4,6},{6,4},{8,10},{10,8},{12,14},{14,12},{16,18},{18,... | collective-permute-start | bytes 884744 | tf_op jit(solution)/shard_map/ppermute | solution.py:401
  144.4 45.1 %collective-permute-start.17 = (bf16[256,4096]{1,0:T(8,128)(2,1)}, bf16[256,4096]{1,0:T(8,128)(2,1)S(1)}, u32[]{:S(2)}, u32[]{:S(2)}) collective-permute-start(bf16[256,4096]{1,0:T(8,128)(2,1)} %collective-permute-done.12.refs_30_), channel_id=1, source_target_pairs={{0,24},{2,26},{4,28},{6,30},{8,0},{10,2},{12,4},{14,6},{16,8},{18,... | collective-permute-start | bytes 6291464 | tf_op jit(solution)/shard_map/ppermute | solution.py:412
  178.5 7.8 %collective-permute-start.16 = (bf16[4,2,256,256]{3,2,1,0:T(8,128)(2,1)}, bf16[4,2,256,256]{3,2,1,0:T(8,128)(2,1)S(1)}, u32[]{:S(2)}, u32[]{:S(2)}) collective-permute-start(bf16[4,2,256,256]{3,2,1,0:T(8,128)(2,1)} %get-tuple-element.120), channel_id=1, source_target_pairs={{0,1},{1,0},{2,3},{3,2},{4,5},{5,4},{6,7},{7,6},{8,9},{9,8},{10,11... | collective-permute-start | bytes 3145736 | tf_op jit(solution)/shard_map/ppermute | solution.py:619
  195.3 16.7 %collective-permute-start.18 = (bf16[1024,256]{1,0:T(8,128)(2,1)S(1)}, bf16[1024,256]{1,0:T(8,128)(2,1)S(1)}, u32[]{:S(2)}, u32[]{:S(2)}) collective-permute-start(bf16[1024,256]{1,0:T(8,128)(2,1)S(1)} %convolution_convert_fusion), channel_id=1, source_target_pairs={{0,1},{2,3},{4,5},{6,7},{9,8},{11,10},{13,12},{15,14},{17,16},{19,... | collective-permute-start | bytes 1572872 | tf_op jit(solution)/shard_map/ppermute | solution.py:628
  196.7 3.2 %collective-permute-start.19 = (bf16[256,128]{1,0:T(8,128)(2,1)S(1)}, bf16[256,128]{1,0:T(8,128)(2,1)S(1)}, u32[]{:S(2)}, u32[]{:S(2)}) collective-permute-start(bf16[256,128]{1,0:T(8,128)(2,1)S(1)} %copy-done.27), channel_id=1, source_target_pairs={{0,2},{2,0},{4,6},{6,4},{8,10},{10,8},{12,14},{14,12},{16,18},{18,... | collective-permute-start | bytes 196616 | tf_op jit(solution)/shard_map/ppermute | solution.py:401
  197.0 3.1 %collective-permute-start.20 = (bf16[256,128]{1,0:T(8,128)(2,1)S(1)}, bf16[256,128]{1,0:T(8,128)(2,1)S(1)}, u32[]{:S(2)}, u32[]{:S(2)}) collective-permute-start(bf16[256,128]{1,0:T(8,128)(2,1)S(1)} %copy-done.26), channel_id=1, source_target_pairs={{0,4},{2,6},{4,0},{6,2},{8,12},{10,14},{12,8},{14,10},{16,20},{18,... | collective-permute-start | bytes 196616 | tf_op jit(solution)/shard_map/ppermute | solution.py:401
  197.3 29.8 %copy-start = (s32[3]{0:T(128)S(1)}, s32[3]{0:T(128)}, u32[]{:S(2)}) copy-start(s32[3]{0:T(128)} %pad_add_fusion.at) | copy-start | bytes 40
  197.3 13.5 %collective-permute-start.24 = (bf16[2,256,256]{2,1,0:T(8,128)(2,1)S(1)}, bf16[2,256,256]{2,1,0:T(8,128)(2,1)S(1)}, u32[]{:S(2)}, u32[]{:S(2)}) collective-permute-start(bf16[2,256,256]{2,1,0:T(8,128)(2,1)S(1)} %get-tuple-element.140), channel_id=1, source_target_pairs={{0,6},{2,4},{4,2},{6,0},{8,14},{10,12},{12,10},{14,8},{16,22},{18,... | collective-permute-start | bytes 786440 | tf_op jit(solution)/shard_map/ppermute | solution.py:401
  199.6 12.4 %collective-permute-start.23 = (bf16[2,256,256]{2,1,0:T(8,128)(2,1)S(1)}, bf16[2,256,256]{2,1,0:T(8,128)(2,1)S(1)}, u32[]{:S(2)}, u32[]{:S(2)}) collective-permute-start(bf16[2,256,256]{2,1,0:T(8,128)(2,1)S(1)} %get-tuple-element.141), channel_id=1, source_target_pairs={{0,4},{2,6},{4,0},{6,2},{8,12},{10,14},{12,8},{14,10},{16,20},{18,... | collective-permute-start | bytes 786440 | tf_op jit(solution)/shard_map/ppermute | solution.py:401
  199.9 12.1 %collective-permute-start.22 = (bf16[2,256,256]{2,1,0:T(8,128)(2,1)S(1)}, bf16[2,256,256]{2,1,0:T(8,128)(2,1)S(1)}, u32[]{:S(2)}, u32[]{:S(2)}) collective-permute-start(bf16[2,256,256]{2,1,0:T(8,128)(2,1)S(1)} %get-tuple-element.142), channel_id=1, source_target_pairs={{0,2},{2,0},{4,6},{6,4},{8,10},{10,8},{12,14},{14,12},{16,18},{18,... | collective-permute-start | bytes 786440 | tf_op jit(solution)/shard_map/ppermute | solution.py:401
  200.1 10.7 %collective-permute-start.21 = (bf16[256,128]{1,0:T(8,128)(2,1)S(1)}, bf16[256,128]{1,0:T(8,128)(2,1)S(1)}, u32[]{:S(2)}, u32[]{:S(2)}) collective-permute-start(bf16[256,128]{1,0:T(8,128)(2,1)S(1)} %copy-done.25), channel_id=1, source_target_pairs={{0,6},{2,4},{4,2},{6,0},{8,14},{10,12},{12,10},{14,8},{16,22},{18,... | collective-permute-start | bytes 196616 | tf_op jit(solution)/shard_map/ppermute | solution.py:401
  212.2 16.6 %collective-permute-start.28 = (f32[2,256,128]{2,1,0:T(8,128)S(1)}, f32[2,256,128]{2,1,0:T(8,128)S(1)}, u32[]{:S(2)}, u32[]{:S(2)}) collective-permute-start(f32[2,256,128]{2,1,0:T(8,128)S(1)} %pad_maximum_fusion), channel_id=1, source_target_pairs={{0,1},{1,0},{2,3},{3,2},{4,5},{5,4},{6,7},{7,6},{8,9},{9,8},{10,11... | collective-permute-start | bytes 786440 | tf_op jit(solution)/shard_map/ppermute | solution.py:658
  215.1 8.4 %collective-permute-start.27 = (bf16[256,256]{1,0:T(8,128)(2,1)S(1)}, bf16[256,256]{1,0:T(8,128)(2,1)S(1)}, u32[]{:S(2)}, u32[]{:S(2)}) collective-permute-start(bf16[256,256]{1,0:T(8,128)(2,1)S(1)} %get-tuple-element.144), channel_id=1, source_target_pairs={{1,7},{3,5},{5,3},{7,1},{8,14},{10,12},{12,10},{14,8},{16,22},{18,... | collective-permute-start | bytes 393224 | tf_op jit(solution)/shard_map/ppermute | solution.py:635
  219.3 5.7 %collective-permute-start.26 = (bf16[256,256]{1,0:T(8,128)(2,1)S(1)}, bf16[256,256]{1,0:T(8,128)(2,1)S(1)}, u32[]{:S(2)}, u32[]{:S(2)}) collective-permute-start(bf16[256,256]{1,0:T(8,128)(2,1)S(1)} %get-tuple-element.145), channel_id=1, source_target_pairs={{1,5},{3,7},{5,1},{7,3},{8,12},{10,14},{12,8},{14,10},{16,20},{18,... | collective-permute-start | bytes 393224 | tf_op jit(solution)/shard_map/ppermute | solution.py:635
  221.4 5.7 %collective-permute-start.25 = (bf16[256,256]{1,0:T(8,128)(2,1)S(1)}, bf16[256,256]{1,0:T(8,128)(2,1)S(1)}, u32[]{:S(2)}, u32[]{:S(2)}) collective-permute-start(bf16[256,256]{1,0:T(8,128)(2,1)S(1)} %get-tuple-element.146), channel_id=1, source_target_pairs={{1,3},{3,1},{5,7},{7,5},{8,10},{10,8},{12,14},{14,12},{16,18},{18,... | collective-permute-start | bytes 393224 | tf_op jit(solution)/shard_map/ppermute | solution.py:635
  (25 other events, 141.8 us)
where the time goes:
time: 232 us; the launch traced here: 230 us
  Pallas kernels  96.9 us (42%)
  waiting for transfers between devices  68.2 us (29%)
  starting transfers between devices  49.8 us (21%)
  local copies, waits for them, and re-layouts  6.67 us (3%)
  matrix products  5.78 us (2%)
    pallas_call x13, Pallas kernels, call(): return lambda *operands: fn(*operands, *after)  95.2 us
    ppermute x3, waiting for transfers between devices, turn(): lax.ppermute(value, 'seq', [(s, (s - RING) % n_seq) for s in range(n_seq)])  22.2 us
    ppermute x4, waiting for transfers between devices, along(): lax.ppermute(value, 'seq', [(s, s + d * RING) for s in range(n_seq) if 0...  21.6 us
    ppermute x16, waiting for transfers between devices, swap(): return lax.ppermute(value, 'seq', [(s, s ^ j) for s in range(n_seq)])  20.9 us
    ppermute x16, starting transfers between devices, swap(): return lax.ppermute(value, 'seq', [(s, s ^ j) for s in range(n_seq)])  15.4 us
    ppermute x4, starting transfers between devices, along(): lax.ppermute(value, 'seq', [(s, s + d * RING) for s in range(n_seq) if 0...  13 us
    ppermute x3, starting transfers between devices, local(): lax.ppermute(late[j], both_axes, [(2 * s + owner(s), 2 * (s ^ j) + owner(...  8.37 us
    ppermute x3, starting transfers between devices, turn(): lax.ppermute(value, 'seq', [(s, (s - RING) % n_seq) for s in range(n_seq)])  7.43 us
  transfers between devices with their start and end apart: 29, of which 11 were waited for; matrix products, arithmetic and copies ran while one was open for 0% of the time, Pallas kernels for 40%

commit v1 on v0

--- a/solution.py
+++ b/solution.py
@@ -311,6 +311,20 @@
     for j in range(RING):
         part = total[j * rows : (j + 1) * rows, k * n_rows : (k + 1) * n_rows]
         tile[j, slot] = part.astype(tile.dtype)
+
+
+def product_kernel(at, acts, w, out, total):
+    g = pl.program_id(0)
+
+    @pl.when(g == 0)
+    def _():
+        total[...] = jnp.zeros_like(total)
+
+    total[...] += mm(acts[...], w[...], NT)
+
+    @pl.when(g == pl.num_programs(0) - 1)
+    def _():
+        out[...] = total[...].astype(out.dtype)
 
 
 def read_kernel(n_heads, at, *refs):
@@ -481,22 +495,15 @@
             [shape((rows, columns), bf16), state_shape, log_shape, cum_shape],
             [cum_t_scratch],
             after,
-            flops=2 * rows * rows * columns * 16 if j else 0,
         )(at, top, bottom, *([top, bottom] * 3))
 
+    parts = [parts[0]] + [swap(parts[j], j) for j in range(1, RING)]
     results = [block(0, packed, packed)]
-    from_x, from_y = swap(packed, 1), swap(packed, 2)
-    results.append(block(1, from_x, from_x, after=[w_first, read_local]))
-    results.append(block(2, from_y, from_y))
-    from_x, from_y, parts = lax.optimization_barrier((from_x, from_y, parts))
-    parts = [parts[0]] + [swap(parts[j], j) for j in range(1, RING)]
-    logs = [v[2] for v in results]
-    from_x, from_y, logs, parts = lax.optimization_barrier((from_x, from_y, logs, parts))
-    blocks = [(packed, packed), (from_x, from_x), (from_y, from_y)]
-    blocks.append((swap(from_x[:half], 2), swap(from_y[half:], 1)))
-    results.append(block(RING - 1, *blocks[-1]))
-    logs.append(results[-1][2])
-    local_acts, fronts, _, cums = zip(*results)
+    logs = [results[0][2]]
+    packed, parts, logs, read_local, w_first = lax.optimization_barrier(
+        (packed, parts, logs, read_local, w_first)
+    )
+    from_x, from_y = lax.optimization_barrier((swap(packed, 1), swap(packed, 2)))
 
     def combine():
         return call(
@@ -519,28 +526,40 @@
             after=after,
         )(at, *pairs)
 
-    w_pieces = [w_in, w_first]
-    while len(w_pieces) < outer - 1:
-        w_pieces.append(turn(w_pieces[-1]))
     state_span, grad_span = combine()
     d = 1
     while d < outer:
         state_got, grad_got = along(state_span, d), along(grad_span, -d)
+        if 2 * d >= outer:
+            w_pieces = [w_in, w_first]
+            while len(w_pieces) < outer - 1:
+                w_pieces.append(turn(w_pieces[-1]))
+            blocks = [(packed, packed), (from_x, from_x), (from_y, from_y)]
+            blocks.append((swap(from_x[:half], 2), swap(from_y[half:], 1)))
+            results.append(block(1, *blocks[1]))
+            results.append(block(2, *blocks[2], after=[w_pieces[-1]]))
+            logs += [v[2] for v in results[1:]]
         if d == 1:
             state_part, grad_part = state_got, grad_got
         else:
-            after = [logs[-1]] if 2 * d >= outer else []
             state_part, grad_part = merge(
-                state_part, state_got, grad_part, grad_got, after=after
+                state_part, state_got, grad_part, grad_got, after=logs[1:]
             )
         if 2 * d < outer:
             state_span, grad_span = merge(state_span, state_got, grad_span, grad_got)
+            if 4 * d >= outer:
+                state_span, grad_span, w_first = lax.optimization_barrier(
+                    (state_span, grad_span, w_first)
+                )
         d *= 2
     grad_part, w_last = lax.optimization_barrier((grad_part, w_pieces[-1]))
     w_last = turn(w_last)
     if not two:
         w_pieces.append(w_last)
     grad_parts = [grad_part] + [swap(grad_part, j) for j in range(1, RING)]
+    results.append(block(RING - 1, *blocks[-1]))
+    logs.append(results[-1][2])
+    local_acts, fronts, _, cums = zip(*results)
 
     ring_grads = call(
         ring_kernel,
@@ -578,7 +597,6 @@
         ]
         + [shape(v, bf16) for v in tile_shapes],
         [pltpu.VMEM((RING * rows, w_total), f32)],
-        flops=2 * RING * rows * columns * w_total,
     )(
         at,
         *local_acts,
@@ -613,13 +631,20 @@
         *parts,
         state_part,
     )
-    read_got = [swap(read_parts[j], j) for j in range(1, RING)]
     if two:
         mine, theirs = tiles
         got = lax.ppermute(theirs, "head", [(0, 1), (1, 0)])
         early = (mine.astype(f32) + got.astype(f32)).astype(bf16)
-        early, read_own, w_last = lax.optimization_barrier((early, read_parts[0], w_last))
-        late = mm(acts, w_last, NT).astype(bf16)
+        late = call(
+            product_kernel,
+            "late_product",
+            (RING,),
+            [tall, pl.BlockSpec((w_rows, part), lambda g, q: (0, g))],
+            const(RING * rows, w_rows),
+            shape((RING * rows, w_rows), bf16),
+            [pltpu.VMEM((RING * rows, w_rows), f32)],
+            after=[early, read_parts[0]],
+        )(at, acts, w_last)
 
         def owner(s):
             return (s // RING + outer - 1) % outer // share
@@ -629,7 +654,7 @@
             late, both_axes, [(2 * s + 1 - owner(s), 2 * s + owner(s)) for s in range(n_seq)]
         )
         early_sent = to_owners(early)
-        got, read_got, early_sent = lax.optimization_barrier((got, read_got, early_sent))
+        got, early_sent = lax.optimization_barrier((got, early_sent))
         late = (late.astype(f32) + got.astype(f32)).astype(bf16).reshape(RING, rows, w_rows)
         late = [late[0]] + [
             lax.ppermute(
@@ -652,6 +677,7 @@
         summed = lax.psum_scatter(tiles[0], "head", scatter_dimension=1, tiled=True)
         pieces = jnp.take(jnp.stack(to_owners(summed)), p ^ jnp.arange(RING), axis=0)
         input_grad = pieces.transpose(2, 1, 0, 3).reshape(rows, share * RING * w_rows)
+    read_got = [swap(read_parts[j], j) for j in range(1, RING)]
     read_carry = read_parts[0].astype(f32) + sum(v.astype(f32) for v in read_got)
     both = jnp.stack([write_local + write_carry, read_local + read_carry])
     if n_head == 2:

time: 232 us -> 240 us (1.034)
  Pallas kernels: 96.9 us -> 104 us
  matrix products: 5.78 us -> 0 us
    ppermute x16, waiting for transfers between devices: 20.9 us -> 46.2 us  [swap(): return lax.ppermute(value, 'seq', [(s, s ^ j) for s in range(n_seq)])]
    ppermute x3, waiting for transfers between devices: 22.2 us -> 9.63 us  [turn(): lax.ppermute(value, 'seq', [(s, (s - RING) % n_seq) for s in range(n_seq)])]
    ppermute x4, waiting for transfers between devices: 21.6 us -> 12.1 us  [along(): lax.ppermute(value, 'seq', [(s, s + d * RING) for s in range(n_seq) if 0...]
    pallas_call x13 -> x14, Pallas kernels: 95.2 us -> 103 us  [call(): return lambda *operands: fn(*operands, *after)]
    ppermute x3, starting transfers between devices: 7.43 us -> 13.3 us  [turn(): lax.ppermute(value, 'seq', [(s, (s - RING) % n_seq) for s in range(n_seq)])]
    dot_general x1 -> x0, matrix products: 5.78 us -> none  [mm(): return lax.dot_general(a, b, dims, preferred_element_type=f32)]
    ppermute x4, starting transfers between devices: 13 us -> 7.56 us  [along(): lax.ppermute(value, 'seq', [(s, s + d * RING) for s in range(n_seq) if 0...]
    unnamed x56 -> x50, local copies, waits for them, and re-layouts: 5.7 us -> 6.05 us
  transfers between devices with their start and end apart: 29 -> 29, of which waited for: 11 -> 14; matrix products, arithmetic and copies ran while one was open for 0% -> 2% of each run, Pallas kernels for 40% -> 40%
where the time goes in v1:
time: 240 us; the launch traced here: 235 us
  Pallas kernels  104 us (43%)
  waiting for transfers between devices  70.3 us (29%)
  starting transfers between devices  48.7 us (20%)
  local copies, waits for them, and re-layouts  8.15 us (3%)
  other arithmetic  2.95 us (1%)
    pallas_call x14, Pallas kernels, call(): return lambda *operands: fn(*operands, *after)  103 us
    ppermute x16, waiting for transfers between devices, swap(): return lax.ppermute(value, 'seq', [(s, s ^ j) for s in range(n_seq)])  46.2 us
    ppermute x16, starting transfers between devices, swap(): return lax.ppermute(value, 'seq', [(s, s ^ j) for s in range(n_seq)])  14.6 us
    ppermute x3, starting transfers between devices, turn(): lax.ppermute(value, 'seq', [(s, (s - RING) % n_seq) for s in range(n_seq)])  13.3 us
    ppermute x4, waiting for transfers between devices, along(): lax.ppermute(value, 'seq', [(s, s + d * RING) for s in range(n_seq) if 0...  12.1 us
    ppermute x3, waiting for transfers between devices, turn(): lax.ppermute(value, 'seq', [(s, (s - RING) % n_seq) for s in range(n_seq)])  9.63 us
    ppermute x3, starting transfers between devices, local(): lax.ppermute(late[j], both_axes, [(2 * s + owner(s), 2 * (s ^ j) + owner(...  8.37 us
    ppermute x4, starting transfers between devices, along(): lax.ppermute(value, 'seq', [(s, s + d * RING) for s in range(n_seq) if 0...  7.56 us
  transfers between devices with their start and end apart: 29, of which 14 were waited for; matrix products, arithmetic and copies ran while one was open for 2% of the time, Pallas kernels for 40%

profile of v1, /device:TPU:1, one launch (start us, length us, event | category | flops | bytes accessed | tf_op | source)
XLA Modules:
  0.0 235.2 jit_solution(14609236579784921908)
XLA Ops:
  0.6 4.2 %collective-permute-start.3 = (bf16[256,4096]{1,0:T(8,128)(2,1)}, bf16[256,4096]{1,0:T(8,128)(2,1)S(1)}, u32[]{:S(2)}, u32[]{:S(2)}) collective-permute-start(bf16[256,4096]{1,0:T(8,128)(2,1)} %refs_28_.1), channel_id=1, source_target_pairs={{0,24},{2,26},{4,28},{6,30},{8,0},{10,2},{12,4},{14,6},{16,8},{18,... | collective-permute-start | bytes 6291464 | tf_op jit(solution)/shard_map/ppermute | solution.py:426
  5.5 8.1 %edges.1 = (bf16[272,1024]{1,0:T(8,128)(2,1)}, bf16[272,1024]{1,0:T(8,128)(2,1)}, bf16[272,1024]{1,0:T(8,128)(2,1)}, bf16[272,1024]{1,0:T(8,128)(2,1)}) custom-call(s32[3]{0:T(128)} %pad_add_fusion.at, bf16[256,4096]{1,0:T(8,128)(2,1)} %refs_31_.1, bf16[256,4096]{1,0:T(8,128)(2,1)} %refs_1_.5, bf16[256,128]{1,0:T(8,128)(2,1)} %refs_2_.5, ...), custom_call_target="tpu_custom_call" | custom-call | tf_op jit(solution)/shard_map/edges/pallas_call | solution.py:395
  16.2 8.2 %own_tokens.1 = (f32[256,128]{1,0:T(8,128)}, f32[256,128]{1,0:T(8,128)}) custom-call(s32[3]{0:T(128)} %pad_add_fusion.at, bf16[256,4096]{1,0:T(8,128)(2,1)} %refs_31_.1, bf16[256,4096]{1,0:T(8,128)(2,1)} %refs_1_.5, bf16[256,128]{1,0:T(8,128)(2,1)} %refs_2_.5, bf16[256,128]{1,0:T(8,128)(2,1)} %refs_3_.3, f32[32,256]{1,0:T(8,128)} %bitcast.21), custom_call_target="tpu_custom_call" | custom-call | tf_op jit(solution)/shard_map/own_tokens/pallas_call | solution.py:395
  24.4 3.8 %pack.1.refs_0_.refs_1_.refs_2_.refs_3_.refs_4_.refs_5_.refs_6_.refs_7_.refs_16_.refs_20_ = bf16[256,4480]{1,0:T(8,128)(2,1)} custom-call(s32[3]{0:T(128)} %pad_add_fusion.at, bf16[256,4096]{1,0:T(8,128)(2,1)} %refs_1_.5, bf16[256,128]{1,0:T(8,128)(2,1)} %refs_2_.5, bf16[256,128]{1,0:T(8,128)(2,1)} %refs_3_.3, f32[32,256]{1,0:T(8,128)} %bitcast.22), custom_call_target="tpu_custom_call" | custom-call | tf_op jit(solution)/shard_map/pack/pallas_call | solution.py:395
  28.3 8.1 %tokens.4 = (bf16[256,4096]{1,0:T(8,128)(2,1)}, bf16[4,128,1024]{2,1,0:T(8,128)(2,1)}, f32[1,4096]{1,0:T(1,128)}, f32[256,128]{1,0:T(8,128)}) custom-call(s32[3]{0:T(128)} %pad_add_fusion.at, bf16[256,4480]{1,0:T(8,128)(2,1)} %pack.1.refs_0_.refs_1_.refs_2_.refs_3_.refs_4_.refs_5_.refs_6_.refs_7_.refs_16_.refs_20_, ...), custom_call_target="tpu_custom_call" | custom-call | tf_op jit(solution)/shard_map/tokens/pallas_call | solution.py:395
  36.4 3.5 %collective-permute-done.2.refs_3_.refs_15_ = bf16[272,1024]{1,0:T(8,128)(2,1)S(1)} collective-permute-done((bf16[272,1024]{1,0:T(8,128)(2,1)}, bf16[272,1024]{1,0:T(8,128)(2,1)S(1)}, u32[]{:S(2)}, u32[]{:S(2)}) %collective-permute-start.2) | collective-permute-done | bytes 557088 | tf_op jit(solution)/shard_map/ppermute | solution.py:415
  39.9 9.5 %collective-permute-done.3.refs_29_ = bf16[256,4096]{1,0:T(8,128)(2,1)S(1)} collective-permute-done((bf16[256,4096]{1,0:T(8,128)(2,1)}, bf16[256,4096]{1,0:T(8,128)(2,1)S(1)}, u32[]{:S(2)}, u32[]{:S(2)}) %collective-permute-start.3) | collective-permute-done | bytes 2097184 | tf_op jit(solution)/shard_map/ppermute | solution.py:426
  53.2 3.4 %messages.1 = (bf16[144,1024]{1,0:T(8,128)(2,1)}, bf16[144,1024]{1,0:T(8,128)(2,1)}) custom-call(s32[3]{0:T(128)} %pad_add_fusion.at, bf16[272,1024]{1,0:T(8,128)(2,1)} %get-tuple-element.76.refs_0_.refs_12_, bf16[272,1024]{1,0:T(8,128)(2,1)} %copy-done.7, bf16[272,1024]{1,0:T(8,128)(2,1)} %copy-done.8, bf16[272,1024]{1,0:T(8,128)(2,1)} %copy-done.9), custom_call_target="tpu_custom_call" | custom-call | tf_op jit(solution)/shard_map/messages/pallas_call | solution.py:395
  56.7 2.0 collective-permute-start.6
  60.0 3.2 %collective-permute-done.6.refs_1_.refs_0_ = bf16[144,1024]{1,0:T(8,128)(2,1)S(1)} collective-permute-done((bf16[144,1024]{1,0:T(8,128)(2,1)}, bf16[144,1024]{1,0:T(8,128)(2,1)S(1)}, u32[]{:S(2)}, u32[]{:S(2)}) %collective-permute-start.6) | collective-permute-done | bytes 294944 | tf_op jit(solution)/shard_map/ppermute | solution.py:418
  63.1 3.7 %collective-permute-done.7.refs_3_.refs_2_ = bf16[144,1024]{1,0:T(8,128)(2,1)S(1)} collective-permute-done((bf16[144,1024]{1,0:T(8,128)(2,1)}, bf16[144,1024]{1,0:T(8,128)(2,1)S(1)}, u32[]{:S(2)}, u32[]{:S(2)}) %collective-permute-start.7) | collective-permute-done | bytes 294944 | tf_op jit(solution)/shard_map/ppermute | solution.py:418
  67.6 2.8 %merge.2 = (bf16[144,1024]{1,0:T(8,128)(2,1)}, bf16[144,1024]{1,0:T(8,128)(2,1)}) custom-call(s32[3]{0:T(128)} %pad_add_fusion.at, bf16[144,1024]{1,0:T(8,128)(2,1)} %get-tuple-element.80.refs_0_, bf16[144,1024]{1,0:T(8,128)(2,1)} %copy-done.13, bf16[144,1024]{1,0:T(8,128)(2,1)} %get-tuple-element.81.refs_2_, bf16[144,1024]{1,0:T(8,128)(2,1)} %copy-done.14), custom_call_target="tpu_custom_call" | custom-call | tf_op jit(solution)/shard_map/merge/pallas_call | solution.py:395
  70.5 3.2 %collective-permute-start.8 = (bf16[256,4096]{1,0:T(8,128)(2,1)}, bf16[256,4096]{1,0:T(8,128)(2,1)}, u32[]{:S(2)}, u32[]{:S(2)}) collective-permute-start(bf16[256,4096]{1,0:T(8,128)(2,1)} %copy-done.10), channel_id=1, source_target_pairs={{0,24},{2,26},{4,28},{6,30},{8,0},{10,2},{12,4},{14,6},{16,8},{18,... | collective-permute-start | bytes 6291464 | tf_op jit(solution)/shard_map/ppermute | solution.py:426
  73.6 27.0 %collective-permute-done.5.refs_0_.refs_1_.refs_2_.refs_3_.refs_4_.refs_5_.refs_6_.refs_7_.refs_18_.refs_22_ = bf16[256,4480]{1,0:T(8,128)(2,1)S(1)} collective-permute-done((bf16[256,4480]{1,0:T(8,128)(2,1)S(1)}, bf16[256,4480]{1,0:T(8,128)(2,1)S(1)}, u32[]{:S(2)}, u32[]{:S(2)}) %collective-permute-start.5) | collective-permute-done | bytes 2293792 | tf_op jit(solution)/shard_map/ppermute | solution.py:415
  104.5 3.0 %collective-permute-start.11 = (bf16[144,1024]{1,0:T(8,128)(2,1)}, bf16[144,1024]{1,0:T(8,128)(2,1)S(1)}, u32[]{:S(2)}, u32[]{:S(2)}) collective-permute-start(bf16[144,1024]{1,0:T(8,128)(2,1)} %get-tuple-element.100), channel_id=1, source_target_pairs={{0,16},{2,18},{4,20},{6,22},{8,24},{10,26},{12,28},{14,30},{1,17},... | collective-permute-start | bytes 884744 | tf_op jit(solution)/shard_map/ppermute | solution.py:418
  108.8 8.0 %tokens.5 = (bf16[256,4096]{1,0:T(8,128)(2,1)}, bf16[4,128,1024]{2,1,0:T(8,128)(2,1)}, f32[1,4096]{1,0:T(1,128)}, f32[256,128]{1,0:T(8,128)}) custom-call(s32[3]{0:T(128)} %pad_add_fusion.at, bf16[256,4480]{1,0:T(8,128)(2,1)} %copy-done.3, bf16[256,4480]{1,0:T(8,128)(2,1)} %copy-done.3, bf16[256,4480]{1,0:T(8,128)(2,1)} %copy-done.3, ...), custom_call_target="tpu_custom_call" | custom-call | tf_op jit(solution)/shard_map/tokens/pallas_call | solution.py:395
  116.9 8.0 %tokens.6 = (bf16[256,4096]{1,0:T(8,128)(2,1)}, bf16[4,128,1024]{2,1,0:T(8,128)(2,1)}, f32[1,4096]{1,0:T(1,128)}, f32[256,128]{1,0:T(8,128)}) custom-call(s32[3]{0:T(128)} %pad_add_fusion.at, bf16[256,4480]{1,0:T(8,128)(2,1)} %copy-done.2, bf16[256,4480]{1,0:T(8,128)(2,1)} %copy-done.2, bf16[256,4480]{1,0:T(8,128)(2,1)} %copy-done.2, ...), custom_call_target="tpu_custom_call" | custom-call | tf_op jit(solution)/shard_map/tokens/pallas_call | solution.py:395
  124.9 5.1 %collective-permute-done.12.refs_3_ = bf16[144,1024]{1,0:T(8,128)(2,1)S(1)} collective-permute-done((bf16[144,1024]{1,0:T(8,128)(2,1)S(1)}, bf16[144,1024]{1,0:T(8,128)(2,1)S(1)}, u32[]{:S(2)}, u32[]{:S(2)}) %collective-permute-start.12) | collective-permute-done | bytes 294944 | tf_op jit(solution)/shard_map/ppermute | solution.py:418
  130.7 2.8 %merge.3 = (bf16[144,1024]{1,0:T(8,128)(2,1)}, bf16[144,1024]{1,0:T(8,128)(2,1)}) custom-call(s32[3]{0:T(128)} %pad_add_fusion.at, bf16[144,1024]{1,0:T(8,128)(2,1)} %copy-done.13, bf16[144,1024]{1,0:T(8,128)(2,1)} %copy-done.20, bf16[144,1024]{1,0:T(8,128)(2,1)} %copy-done.14, bf16[144,1024]{1,0:T(8,128)(2,1)} %copy-done.21, ...), custom_call_target="tpu_custom_call" | custom-call | tf_op jit(solution)/shard_map/merge/pallas_call | solution.py:395
  133.5 5.9 %collective-permute-start.16 = (bf16[256,4096]{1,0:T(8,128)(2,1)}, bf16[256,4096]{1,0:T(8,128)(2,1)S(1)}, u32[]{:S(2)}, u32[]{:S(2)}) collective-permute-start(bf16[256,4096]{1,0:T(8,128)(2,1)} %collective-permute-done.8.refs_8_.refs_30_), channel_id=1, source_target_pairs={{0,24},{2,26},{4,28},{6,30},{8,0},{10,2},{12,4},{14,6},{16,8},{18,... | collective-permute-start | bytes 6291464 | tf_op jit(solution)/shard_map/ppermute | solution.py:426
  143.2 8.0 %tokens.7 = (bf16[256,4096]{1,0:T(8,128)(2,1)}, bf16[4,128,1024]{2,1,0:T(8,128)(2,1)}, f32[1,4096]{1,0:T(1,128)}, f32[256,128]{1,0:T(8,128)}) custom-call(s32[3]{0:T(128)} %pad_add_fusion.at, bf16[128,4480]{1,0:T(8,128)(2,1)} %copy-done.5, bf16[128,4480]{1,0:T(8,128)(2,1)} %copy-done.4, bf16[128,4480]{1,0:T(8,128)(2,1)} %copy-done.5, ...), custom_call_target="tpu_custom_call" | custom-call | tf_op jit(solution)/shard_map/tokens/pallas_call | solution.py:395
  151.1 6.1 %ring_grads.1 = (bf16[4,128,1024]{2,1,0:T(8,128)(2,1)}, bf16[4,128,1024]{2,1,0:T(8,128)(2,1)}, bf16[4,128,1024]{2,1,0:T(8,128)(2,1)}, bf16[4,128,1024]{2,1,0:T(8,128)(2,1)}) custom-call(s32[3]{0:T(128)} %pad_add_fusion.at, bf16[4,128,1024]{2,1,0:T(8,128)(2,1)} %get-tuple-element.88.refs_0_, bf16[4,128,1024]{2,1,0:T(8,128)(2,1)} %get-tuple-element.89.refs_1_, ...), custom_call_target="tpu_custom_call" | custom-call | tf_op jit(solution)/shard_map/ring_grads/pallas_call | solution.py:395
  158.2 21.1 %finish.1 = (bf16[1024,4096]{1,0:T(8,128)(2,1)}, bf16[256,4096]{1,0:T(8,128)(2,1)}, f32[256,128]{1,0:T(8,128)}, bf16[4,2,256,256]{3,2,1,0:T(8,128)(2,1)}, bf16[4,2,256,256]{3,2,1,0:T(8,128)(2,1)}) custom-call(s32[3]{0:T(128)} %pad_add_fusion.at, bf16[256,4096]{1,0:T(8,128)(2,1)} %get-tuple-element.65.refs_0_, bf16[256,4096]{1,0:T(8,128)(2,1)} %get-tuple-element.74.refs_1_, ...), custom_call_target="tpu_custom_call" | custom-call | tf_op jit(solution)/shard_map/finish/pallas_call | solution.py:395
  181.0 6.5 %read_carry.1 = (bf16[256,128]{1,0:T(8,128)(2,1)}, bf16[256,128]{1,0:T(8,128)(2,1)}, bf16[256,128]{1,0:T(8,128)(2,1)}, bf16[256,128]{1,0:T(8,128)(2,1)}) custom-call(s32[3]{0:T(128)} %pad_add_fusion.at, bf16[256,4480]{1,0:T(8,128)(2,1)} %pack.1.refs_0_.refs_1_.refs_2_.refs_3_.refs_4_.refs_5_.refs_6_.refs_7_.refs_16_.refs_20_, bf16[256,4480]{1,0:T(8,128)(2,1)} %copy-done.3, ...), custom_call_target="tpu_custom_call" | custom-call | tf_op jit(solution)/shard_map/read_carry/pallas_call | solution.py:395
  196.2 7.5 %late_product.1 = bf16[1024,256]{1,0:T(8,128)(2,1)} custom-call(s32[3]{0:T(128)} %pad_add_fusion.at, bf16[1024,4096]{1,0:T(8,128)(2,1)} %get-tuple-element.108.refs_0_, bf16[256,4096]{1,0:T(8,128)(2,1)} %copy-done.12, bf16[4,2,256,256]{3,2,1,0:T(8,128)(2,1)} %add_convert_fusion.refs_2_, bf16[256,128]{1,0:T(8,128)(2,1)} %get-tuple-element.114.refs_3_), custom_call_target="tpu_custom_call" | custom-call | tf_op jit(solution)/shard_map/late_product/pallas_call | solution.py:395
  207.0 1.8 collective-permute-start.21
  209.8 6.2 %collective-permute-done.21.refs_3_ = bf16[2,256,256]{2,1,0:T(8,128)(2,1)S(1)} collective-permute-done((bf16[2,256,256]{2,1,0:T(8,128)(2,1)S(1)}, bf16[2,256,256]{2,1,0:T(8,128)(2,1)S(1)}, u32[]{:S(2)}, u32[]{:S(2)}) %collective-permute-start.21) | collective-permute-done | bytes 262176 | tf_op jit(solution)/shard_map/ppermute | solution.py:415
  215.9 5.9 %collective-permute-done.20.refs_2_ = bf16[2,256,256]{2,1,0:T(8,128)(2,1)S(1)} collective-permute-done((bf16[2,256,256]{2,1,0:T(8,128)(2,1)S(1)}, bf16[2,256,256]{2,1,0:T(8,128)(2,1)S(1)}, u32[]{:S(2)}, u32[]{:S(2)}) %collective-permute-start.20) | collective-permute-done | bytes 262176 | tf_op jit(solution)/shard_map/ppermute | solution.py:415
  222.1 3.1 %collective-permute-start.24 = (bf16[256,256]{1,0:T(8,128)(2,1)S(1)}, bf16[256,256]{1,0:T(8,128)(2,1)S(1)}, u32[]{:S(2)}, u32[]{:S(2)}) collective-permute-start(bf16[256,256]{1,0:T(8,128)(2,1)S(1)} %get-tuple-element.130), channel_id=1, source_target_pairs={{1,7},{3,5},{5,3},{7,1},{8,14},{10,12},{12,10},{14,8},{16,22},{18,... | collective-permute-start | bytes 393224 | tf_op jit(solution)/shard_map/ppermute | solution.py:660
  225.2 2.7 %collective-permute-start.23 = (bf16[256,256]{1,0:T(8,128)(2,1)S(1)}, bf16[256,256]{1,0:T(8,128)(2,1)S(1)}, u32[]{:S(2)}, u32[]{:S(2)}) collective-permute-start(bf16[256,256]{1,0:T(8,128)(2,1)S(1)} %get-tuple-element.131), channel_id=1, source_target_pairs={{1,5},{3,7},{5,1},{7,3},{8,12},{10,14},{12,8},{14,10},{16,20},{18,... | collective-permute-start | bytes 393224 | tf_op jit(solution)/shard_map/ppermute | solution.py:660
  227.8 2.6 %collective-permute-start.22 = (bf16[256,256]{1,0:T(8,128)(2,1)S(1)}, bf16[256,256]{1,0:T(8,128)(2,1)S(1)}, u32[]{:S(2)}, u32[]{:S(2)}) collective-permute-start(bf16[256,256]{1,0:T(8,128)(2,1)S(1)} %get-tuple-element.132), channel_id=1, source_target_pairs={{1,3},{3,1},{5,7},{7,5},{8,10},{10,8},{12,14},{14,12},{16,18},{18,... | collective-permute-start | bytes 393224 | tf_op jit(solution)/shard_map/ppermute | solution.py:660
  231.2 2.4 %collective-permute-done.22.refs_5_ = bf16[256,256]{1,0:T(8,128)(2,1)S(1)} collective-permute-done((bf16[256,256]{1,0:T(8,128)(2,1)S(1)}, bf16[256,256]{1,0:T(8,128)(2,1)S(1)}, u32[]{:S(2)}, u32[]{:S(2)}) %collective-permute-start.22) | collective-permute-done | bytes 131104 | tf_op jit(solution)/shard_map/ppermute | solution.py:660
  (103 shorter events, 36.7 us)
Async XLA Ops:
  0.6 48.8 %collective-permute-start.3 = (bf16[256,4096]{1,0:T(8,128)(2,1)}, bf16[256,4096]{1,0:T(8,128)(2,1)S(1)}, u32[]{:S(2)}, u32[]{:S(2)}) collective-permute-start(bf16[256,4096]{1,0:T(8,128)(2,1)} %refs_28_.1), channel_id=1, source_target_pairs={{0,24},{2,26},{4,28},{6,30},{8,0},{10,2},{12,4},{14,6},{16,8},{18,... | collective-permute-start | bytes 6291464 | tf_op jit(solution)/shard_map/ppermute | solution.py:426
  13.6 22.8 %collective-permute-start = (bf16[272,1024]{1,0:T(8,128)(2,1)}, bf16[272,1024]{1,0:T(8,128)(2,1)S(1)}, u32[]{:S(2)}, u32[]{:S(2)}) collective-permute-start(bf16[272,1024]{1,0:T(8,128)(2,1)} %get-tuple-element.67), channel_id=1, source_target_pairs={{0,2},{2,0},{4,6},{6,4},{8,10},{10,8},{12,14},{14,12},{16,18},{18,... | collective-permute-start | bytes 1671176 | tf_op jit(solution)/shard_map/ppermute | solution.py:415
  14.8 21.6 %collective-permute-start.1 = (bf16[272,1024]{1,0:T(8,128)(2,1)}, bf16[272,1024]{1,0:T(8,128)(2,1)S(1)}, u32[]{:S(2)}, u32[]{:S(2)}) collective-permute-start(bf16[272,1024]{1,0:T(8,128)(2,1)} %get-tuple-element.68), channel_id=1, source_target_pairs={{0,4},{2,6},{4,0},{6,2},{8,12},{10,14},{12,8},{14,10},{16,20},{18,... | collective-permute-start | bytes 1671176 | tf_op jit(solution)/shard_map/ppermute | solution.py:415
  16.0 23.9 %collective-permute-start.2 = (bf16[272,1024]{1,0:T(8,128)(2,1)}, bf16[272,1024]{1,0:T(8,128)(2,1)S(1)}, u32[]{:S(2)}, u32[]{:S(2)}) collective-permute-start(bf16[272,1024]{1,0:T(8,128)(2,1)} %get-tuple-element.69), channel_id=1, source_target_pairs={{0,6},{2,4},{4,2},{6,0},{8,14},{10,12},{12,10},{14,8},{16,22},{18,... | collective-permute-start | bytes 1671176 | tf_op jit(solution)/shard_map/ppermute | solution.py:415
  28.3 22.5 %copy-start.1 = (bf16[256,4480]{1,0:T(8,128)(2,1)S(1)}, bf16[256,4480]{1,0:T(8,128)(2,1)}, u32[]{:S(2)}) copy-start(bf16[256,4480]{1,0:T(8,128)(2,1)} %pack.1.refs_0_.refs_1_.refs_2_.refs_3_.refs_4_.refs_5_.refs_6_.refs_7_.refs_16_.refs_20_) | copy-start | bytes 6881284
  50.8 49.9 %collective-permute-start.5 = (bf16[256,4480]{1,0:T(8,128)(2,1)S(1)}, bf16[256,4480]{1,0:T(8,128)(2,1)S(1)}, u32[]{:S(2)}, u32[]{:S(2)}) collective-permute-start(bf16[256,4480]{1,0:T(8,128)(2,1)S(1)} %copy-done.1), channel_id=1, source_target_pairs={{0,4},{2,6},{4,0},{6,2},{8,12},{10,14},{12,8},{14,10},{16,20},{18,... | collective-permute-start | bytes 6881288 | tf_op jit(solution)/shard_map/ppermute | solution.py:415
  52.0 49.6 %collective-permute-start.4 = (bf16[256,4480]{1,0:T(8,128)(2,1)S(1)}, bf16[256,4480]{1,0:T(8,128)(2,1)S(1)}, u32[]{:S(2)}, u32[]{:S(2)}) collective-permute-start(bf16[256,4480]{1,0:T(8,128)(2,1)S(1)} %copy-done.1), channel_id=1, source_target_pairs={{0,2},{2,0},{4,6},{6,4},{8,10},{10,8},{12,14},{14,12},{16,18},{18,... | collective-permute-start | bytes 6881288 | tf_op jit(solution)/shard_map/ppermute | solution.py:415
  56.7 6.5 %collective-permute-start.6 = (bf16[144,1024]{1,0:T(8,128)(2,1)}, bf16[144,1024]{1,0:T(8,128)(2,1)S(1)}, u32[]{:S(2)}, u32[]{:S(2)}) collective-permute-start(bf16[144,1024]{1,0:T(8,128)(2,1)} %get-tuple-element.80.refs_0_), channel_id=1, source_target_pairs={{0,8},{2,10},{4,12},{6,14},{8,16},{10,18},{12,20},{14,22},{16,24},... | collective-permute-start | bytes 884744 | tf_op jit(solution)/shard_map/ppermute | solution.py:418
  58.7 8.2 %collective-permute-start.7 = (bf16[144,1024]{1,0:T(8,128)(2,1)}, bf16[144,1024]{1,0:T(8,128)(2,1)S(1)}, u32[]{:S(2)}, u32[]{:S(2)}) collective-permute-start(bf16[144,1024]{1,0:T(8,128)(2,1)} %get-tuple-element.81.refs_2_), channel_id=1, source_target_pairs={{8,0},{10,2},{12,4},{14,6},{16,8},{18,10},{20,12},{22,14},{24,16},... | collective-permute-start | bytes 884744 | tf_op jit(solution)/shard_map/ppermute | solution.py:418
  70.5 37.0 %copy-start.24 = (bf16[144,1024]{1,0:T(8,128)(2,1)S(1)}, bf16[144,1024]{1,0:T(8,128)(2,1)}, u32[]{:S(2)}) copy-start(bf16[144,1024]{1,0:T(8,128)(2,1)} %get-tuple-element.101) | copy-start | bytes 884740
  70.5 46.4 %collective-permute-start.8 = (bf16[256,4096]{1,0:T(8,128)(2,1)}, bf16[256,4096]{1,0:T(8,128)(2,1)}, u32[]{:S(2)}, u32[]{:S(2)}) collective-permute-start(bf16[256,4096]{1,0:T(8,128)(2,1)} %copy-done.10), channel_id=1, source_target_pairs={{0,24},{2,26},{4,28},{6,30},{8,0},{10,2},{12,4},{14,6},{16,8},{18,... | collective-permute-start | bytes 6291464 | tf_op jit(solution)/shard_map/ppermute | solution.py:426
  102.8 38.1 %collective-permute-start.10 = (bf16[128,4480]{1,0:T(8,128)(2,1)}, bf16[128,4480]{1,0:T(8,128)(2,1)S(1)}, u32[]{:S(2)}, u32[]{:S(2)}) collective-permute-start(bf16[128,4480]{1,0:T(8,128)(2,1)} %slice.41), channel_id=1, source_target_pairs={{0,2},{2,0},{4,6},{6,4},{8,10},{10,8},{12,14},{14,12},{16,18},{18,... | collective-permute-start | bytes 3440648 | tf_op jit(solution)/shard_map/ppermute | solution.py:415
  104.1 38.0 %collective-permute-start.9 = (bf16[128,4480]{1,0:T(8,128)(2,1)S(1)}, bf16[128,4480]{1,0:T(8,128)(2,1)S(1)}, u32[]{:S(2)}, u32[]{:S(2)}) collective-permute-start(bf16[128,4480]{1,0:T(8,128)(2,1)S(1)} %slice.40), channel_id=1, source_target_pairs={{0,4},{2,6},{4,0},{6,2},{8,12},{10,14},{12,8},{14,10},{16,20},{18,... | collective-permute-start | bytes 3440648 | tf_op jit(solution)/shard_map/ppermute | solution.py:415
  104.5 20.4 %collective-permute-start.11 = (bf16[144,1024]{1,0:T(8,128)(2,1)}, bf16[144,1024]{1,0:T(8,128)(2,1)S(1)}, u32[]{:S(2)}, u32[]{:S(2)}) collective-permute-start(bf16[144,1024]{1,0:T(8,128)(2,1)} %get-tuple-element.100), channel_id=1, source_target_pairs={{0,16},{2,18},{4,20},{6,22},{8,24},{10,26},{12,28},{14,30},{1,17},... | collective-permute-start | bytes 884744 | tf_op jit(solution)/shard_map/ppermute | solution.py:418
  107.5 22.6 %collective-permute-start.12 = (bf16[144,1024]{1,0:T(8,128)(2,1)S(1)}, bf16[144,1024]{1,0:T(8,128)(2,1)S(1)}, u32[]{:S(2)}, u32[]{:S(2)}) collective-permute-start(bf16[144,1024]{1,0:T(8,128)(2,1)S(1)} %copy-done.24), channel_id=1, source_target_pairs={{16,0},{18,2},{20,4},{22,6},{24,8},{26,10},{28,12},{30,14},{17,1},... | collective-permute-start | bytes 884744 | tf_op jit(solution)/shard_map/ppermute | solution.py:418
  133.5 61.4 %collective-permute-start.16 = (bf16[256,4096]{1,0:T(8,128)(2,1)}, bf16[256,4096]{1,0:T(8,128)(2,1)S(1)}, u32[]{:S(2)}, u32[]{:S(2)}) collective-permute-start(bf16[256,4096]{1,0:T(8,128)(2,1)} %collective-permute-done.8.refs_8_.refs_30_), channel_id=1, source_target_pairs={{0,24},{2,26},{4,28},{6,30},{8,0},{10,2},{12,4},{14,6},{16,8},{18,... | collective-permute-start | bytes 6291464 | tf_op jit(solution)/shard_map/ppermute | solution.py:426
  139.5 17.8 %collective-permute-start.15 = (bf16[144,1024]{1,0:T(8,128)(2,1)}, bf16[144,1024]{1,0:T(8,128)(2,1)S(1)}, u32[]{:S(2)}, u32[]{:S(2)}) collective-permute-start(bf16[144,1024]{1,0:T(8,128)(2,1)} %get-tuple-element.103.refs_8_), channel_id=1, source_target_pairs={{0,6},{2,4},{4,2},{6,0},{8,14},{10,12},{12,10},{14,8},{16,22},{18,... | collective-permute-start | bytes 884744 | tf_op jit(solution)/shard_map/ppermute | solution.py:415
  139.7 17.6 %collective-permute-start.14 = (bf16[144,1024]{1,0:T(8,128)(2,1)}, bf16[144,1024]{1,0:T(8,128)(2,1)S(1)}, u32[]{:S(2)}, u32[]{:S(2)}) collective-permute-start(bf16[144,1024]{1,0:T(8,128)(2,1)} %get-tuple-element.103.refs_8_), channel_id=1, source_target_pairs={{0,4},{2,6},{4,0},{6,2},{8,12},{10,14},{12,8},{14,10},{16,20},{18,... | collective-permute-start | bytes 884744 | tf_op jit(solution)/shard_map/ppermute | solution.py:415
  140.9 16.4 %collective-permute-start.13 = (bf16[144,1024]{1,0:T(8,128)(2,1)}, bf16[144,1024]{1,0:T(8,128)(2,1)S(1)}, u32[]{:S(2)}, u32[]{:S(2)}) collective-permute-start(bf16[144,1024]{1,0:T(8,128)(2,1)} %get-tuple-element.103.refs_8_), channel_id=1, source_target_pairs={{0,2},{2,0},{4,6},{6,4},{8,10},{10,8},{12,14},{14,12},{16,18},{18,... | collective-permute-start | bytes 884744 | tf_op jit(solution)/shard_map/ppermute | solution.py:415
  179.4 14.3 %collective-permute-start.17 = (bf16[4,2,256,256]{3,2,1,0:T(8,128)(2,1)}, bf16[4,2,256,256]{3,2,1,0:T(8,128)(2,1)S(1)}, u32[]{:S(2)}, u32[]{:S(2)}) collective-permute-start(bf16[4,2,256,256]{3,2,1,0:T(8,128)(2,1)} %get-tuple-element.111), channel_id=1, source_target_pairs={{0,1},{1,0},{2,3},{3,2},{4,5},{5,4},{6,7},{7,6},{8,9},{9,8},{10,11... | collective-permute-start | bytes 3145736 | tf_op jit(solution)/shard_map/ppermute | solution.py:636
  187.5 3.9 %collective-permute-start.25 = (bf16[256,128]{1,0:T(8,128)(2,1)}, bf16[256,128]{1,0:T(8,128)(2,1)S(1)}, u32[]{:S(2)}, u32[]{:S(2)}) collective-permute-start(bf16[256,128]{1,0:T(8,128)(2,1)} %get-tuple-element.123), channel_id=1, source_target_pairs={{0,2},{2,0},{4,6},{6,4},{8,10},{10,8},{12,14},{14,12},{16,18},{18,... | collective-permute-start | bytes 196616 | tf_op jit(solution)/shard_map/ppermute | solution.py:415
  188.2 3.6 %collective-permute-start.26 = (bf16[256,128]{1,0:T(8,128)(2,1)}, bf16[256,128]{1,0:T(8,128)(2,1)S(1)}, u32[]{:S(2)}, u32[]{:S(2)}) collective-permute-start(bf16[256,128]{1,0:T(8,128)(2,1)} %get-tuple-element.124), channel_id=1, source_target_pairs={{0,4},{2,6},{4,0},{6,2},{8,12},{10,14},{12,8},{14,10},{16,20},{18,... | collective-permute-start | bytes 196616 | tf_op jit(solution)/shard_map/ppermute | solution.py:415
  188.4 4.3 %collective-permute-start.27 = (bf16[256,128]{1,0:T(8,128)(2,1)}, bf16[256,128]{1,0:T(8,128)(2,1)S(1)}, u32[]{:S(2)}, u32[]{:S(2)}) collective-permute-start(bf16[256,128]{1,0:T(8,128)(2,1)} %get-tuple-element.125), channel_id=1, source_target_pairs={{0,6},{2,4},{4,2},{6,0},{8,14},{10,12},{12,10},{14,8},{16,22},{18,... | collective-permute-start | bytes 196616 | tf_op jit(solution)/shard_map/ppermute | solution.py:415
  203.7 18.1 %collective-permute-start.18 = (bf16[1024,256]{1,0:T(8,128)(2,1)}, bf16[1024,256]{1,0:T(8,128)(2,1)S(1)}, u32[]{:S(2)}, u32[]{:S(2)}) collective-permute-start(bf16[1024,256]{1,0:T(8,128)(2,1)} %late_product.1), channel_id=1, source_target_pairs={{0,1},{2,3},{4,5},{6,7},{9,8},{11,10},{13,12},{15,14},{17,16},{19,... | collective-permute-start | bytes 1572872 | tf_op jit(solution)/shard_map/ppermute | solution.py:653
  205.2 4.5 %collective-permute-start.28 = (f32[2,256,128]{2,1,0:T(8,128)S(1)}, f32[2,256,128]{2,1,0:T(8,128)S(1)}, u32[]{:S(2)}, u32[]{:S(2)}) collective-permute-start(f32[2,256,128]{2,1,0:T(8,128)S(1)} %pad_maximum_fusion), channel_id=1, source_target_pairs={{0,1},{1,0},{2,3},{3,2},{4,5},{5,4},{6,7},{7,6},{8,9},{9,8},{10,11... | collective-permute-start | bytes 786440 | tf_op jit(solution)/shard_map/ppermute | solution.py:684
  207.0 26.5 %copy-start = (s32[3]{0:T(128)S(1)}, s32[3]{0:T(128)}, u32[]{:S(2)}) copy-start(s32[3]{0:T(128)} %pad_add_fusion.at) | copy-start | bytes 40
  207.0 8.9 %collective-permute-start.21 = (bf16[2,256,256]{2,1,0:T(8,128)(2,1)S(1)}, bf16[2,256,256]{2,1,0:T(8,128)(2,1)S(1)}, u32[]{:S(2)}, u32[]{:S(2)}) collective-permute-start(bf16[2,256,256]{2,1,0:T(8,128)(2,1)S(1)} %get-tuple-element.126), channel_id=1, source_target_pairs={{0,6},{2,4},{4,2},{6,0},{8,14},{10,12},{12,10},{14,8},{16,22},{18,... | collective-permute-start | bytes 786440 | tf_op jit(solution)/shard_map/ppermute | solution.py:415
  208.8 13.1 %collective-permute-start.20 = (bf16[2,256,256]{2,1,0:T(8,128)(2,1)S(1)}, bf16[2,256,256]{2,1,0:T(8,128)(2,1)S(1)}, u32[]{:S(2)}, u32[]{:S(2)}) collective-permute-start(bf16[2,256,256]{2,1,0:T(8,128)(2,1)S(1)} %get-tuple-element.127), channel_id=1, source_target_pairs={{0,4},{2,6},{4,0},{6,2},{8,12},{10,14},{12,8},{14,10},{16,20},{18,... | collective-permute-start | bytes 786440 | tf_op jit(solution)/shard_map/ppermute | solution.py:415
  209.0 12.8 %collective-permute-start.19 = (bf16[2,256,256]{2,1,0:T(8,128)(2,1)S(1)}, bf16[2,256,256]{2,1,0:T(8,128)(2,1)S(1)}, u32[]{:S(2)}, u32[]{:S(2)}) collective-permute-start(bf16[2,256,256]{2,1,0:T(8,128)(2,1)S(1)} %get-tuple-element.128), channel_id=1, source_target_pairs={{0,2},{2,0},{4,6},{6,4},{8,10},{10,8},{12,14},{14,12},{16,18},{18,... | collective-permute-start | bytes 786440 | tf_op jit(solution)/shard_map/ppermute | solution.py:415
  222.1 9.1 %collective-permute-start.24 = (bf16[256,256]{1,0:T(8,128)(2,1)S(1)}, bf16[256,256]{1,0:T(8,128)(2,1)S(1)}, u32[]{:S(2)}, u32[]{:S(2)}) collective-permute-start(bf16[256,256]{1,0:T(8,128)(2,1)S(1)} %get-tuple-element.130), channel_id=1, source_target_pairs={{1,7},{3,5},{5,3},{7,1},{8,14},{10,12},{12,10},{14,8},{16,22},{18,... | collective-permute-start | bytes 393224 | tf_op jit(solution)/shard_map/ppermute | solution.py:660
  225.2 6.0 %collective-permute-start.23 = (bf16[256,256]{1,0:T(8,128)(2,1)S(1)}, bf16[256,256]{1,0:T(8,128)(2,1)S(1)}, u32[]{:S(2)}, u32[]{:S(2)}) collective-permute-start(bf16[256,256]{1,0:T(8,128)(2,1)S(1)} %get-tuple-element.131), channel_id=1, source_target_pairs={{1,5},{3,7},{5,1},{7,3},{8,12},{10,14},{12,8},{14,10},{16,20},{18,... | collective-permute-start | bytes 393224 | tf_op jit(solution)/shard_map/ppermute | solution.py:660
  227.8 5.7 %collective-permute-start.22 = (bf16[256,256]{1,0:T(8,128)(2,1)S(1)}, bf16[256,256]{1,0:T(8,128)(2,1)S(1)}, u32[]{:S(2)}, u32[]{:S(2)}) collective-permute-start(bf16[256,256]{1,0:T(8,128)(2,1)S(1)} %get-tuple-element.132), channel_id=1, source_target_pairs={{1,3},{3,1},{5,7},{7,5},{8,10},{10,8},{12,14},{14,12},{16,18},{18,... | collective-permute-start | bytes 393224 | tf_op jit(solution)/shard_map/ppermute | solution.py:660
  (22 other events, 138.3 us)
